TPU v7x, 1024 devices: a whole 8x8x8 slice. The times are simulated.
1024 devices in a mesh: gz: 64 (over y, x), ha: 16 (over z, core).
Axes of the slice: x: 8, y: 8, z: 8, core: 2. Of those that a mesh axis runs over, the one named last changes fastest.
Arguments:
- source: float32 [128, 512, 512], P('gz', 'ha'), may hold values from -5 to 5
- faces: float32 [129], replicated, may hold values from 1000 to 8000
Outputs:
- pressure: float32 [128, 512, 512], P('gz', 'ha')
All inputs are finite; a program needn't handle non-finite values.
Results may differ from a plain program's by a relative error of at most 0.00095.
Values sent between devices are 32-bit elements; how exact they have to be, the bound alone decides.
No kernel may reach another device: no remote copies, remote signals or barrier semaphores. Data moves between devices by JAX's collectives and lax.ppermute only.
A program may use at most 128 MiB of HBM per device.

v0:
```python
import math

import jax
import jax.numpy as jnp
from jax import lax
from jax.sharding import PartitionSpec as P

HIGH = lax.Precision.HIGHEST


def hartley(count):
    index = jnp.arange(count, dtype=jnp.int32)
    phase = (index[:, None] * index[None, :] % count).astype(jnp.float32) * (2.0 * math.pi / count)
    return (jnp.cos(phase) + jnp.sin(phase)) / math.sqrt(count)


def eigen(index, count):
    return 2.0 - 2.0 * jnp.cos(index.astype(jnp.float32) * (2.0 * math.pi / count))


def forward_sweep(lower, upper, rhs, shift, start_c, start_d):

    def forward(carry, row):
        cprime, dprime = carry
        low, up, value = row
        pivot = low + up + shift + low * cprime
        cnext = -up / pivot
        dnext = (value + low * dprime) / pivot
        return ((cnext, dnext), (cnext, dnext))

    final, (cseq, dseq) = lax.scan(forward, (start_c, start_d), (lower, upper, rhs))
    return (cseq, dseq)


def back_sweep(cseq, dseq, above):

    def backward(carry, row):
        cvalue, dvalue = row
        value = dvalue - cvalue * carry
        return (value, value)

    final, solved = lax.scan(backward, above, (cseq, dseq), reverse=True)
    return solved


def on_device(source, faces):
    depth, rows, width_x = source.shape
    groups = lax.axis_size("ha")
    slabs = lax.axis_size("gz")
    width_y = rows * groups
    local_x = width_x // groups
    count = local_x * width_y
    hx = hartley(width_x)
    hy = hartley(width_y)
    half = jnp.einsum("zyx,xk->zky", source, hx, precision=HIGH)
    pencils = lax.all_to_all(half, "ha", split_axis=1, concat_axis=2, tiled=True)
    modes = jnp.einsum("zky,yl->zkl", pencils, hy, precision=HIGH)
    first = lax.axis_index("ha") * local_x
    wave_x = first + jnp.arange(local_x, dtype=jnp.int32)
    wave_y = jnp.arange(width_y, dtype=jnp.int32)
    shift = (eigen(wave_x, width_x)[:, None] + eigen(wave_y, width_y)[None, :]).reshape(count)
    rhs = modes.reshape(depth, count)
    share = count // slabs
    blocks = rhs.reshape(depth, slabs, share)
    columns = lax.all_to_all(blocks, "gz", split_axis=1, concat_axis=0, tiled=True)
    local_shift = lax.dynamic_slice_in_dim(shift, lax.axis_index("gz") * share, share)
    zero = jnp.zeros((share,), jnp.float32)
    cseq, dseq = forward_sweep(
        faces[:-1], faces[1:], columns.reshape(depth * slabs, share), local_shift, zero, zero
    )
    solved = back_sweep(cseq, dseq, zero)
    returned = lax.all_to_all(
        solved.reshape(depth * slabs, 1, share), "gz", split_axis=0, concat_axis=1, tiled=True
    )
    solution = returned.reshape(depth, count)
    spectral = solution.reshape(depth, local_x, width_y)
    back = jnp.einsum("zkl,ly->zky", spectral, hy, precision=HIGH)
    grid = lax.all_to_all(back, "ha", split_axis=2, concat_axis=1, tiled=True)
    return jnp.einsum("zky,kx->zyx", grid, hx, precision=HIGH)


def solution(mesh):
    in_specs = (P("gz", "ha", None), P())
    out_specs = P("gz", "ha", None)
    return jax.shard_map(
        on_device, mesh=mesh, in_specs=in_specs, out_specs=out_specs, check_vma=False
    )
```

profile of v0, /device:TPU:1, one launch (start us, length us, event | category | flops | bytes accessed | tf_op | source)
XLA Modules:
  0.0 643.4 jit_solution(4597141231453423077)
XLA Ops:
  0.0 0.9 copy-done
  0.9 5.2 convolution_bitcast_fusion
  6.3 1.2 reshape.32
  7.5 18.2 %all-to-all-start = ((f32[16,1,2048]{2,1,0:T(1,128)}), f32[16,1,2048]{2,1,0:T(1,128)S(1)}, u32[]{:S(2)}, u32[]{:S(2)}) async-start(f32[16,1,2048]{2,1,0:T(1,128)} %reshape.32), calls=%async_computation | async-start | bytes 262144 | tf_op jit(solution)/shard_map/all_to_all | solution.py:56
  25.8 9.1 %all-to-all-done = f32[16,1,2048]{2,1,0:T(1,128)S(1)} async-done(((f32[16,1,2048]{2,1,0:T(1,128)}), f32[16,1,2048]{2,1,0:T(1,128)S(1)}, u32[]{:S(2)}, u32[]{:S(2)}) %all-to-all-start) | async-done | bytes 131104 | tf_op jit(solution)/shard_map/all_to_all | solution.py:56
  35.4 0.9 reduce
  37.3 5.1 fusion.11
  42.4 0.8 copy.9
  43.2 13.2 %all-to-all-start.1 = ((f32[2,64,256]{2,0,1:T(2,128)}), f32[2,64,256]{2,0,1:T(2,128)S(1)}, u32[]{:S(2)}, u32[]{:S(2)}) async-start(f32[2,64,256]{2,0,1:T(2,128)} %copy.9), calls=%async_computation.1 | async-start | bytes 262144 | tf_op jit(solution)/shard_map/all_to_all | solution.py:65
  57.2 11.2 %all-to-all-done.1 = f32[2,64,256]{2,0,1:T(2,128)S(1)} async-done(((f32[2,64,256]{2,0,1:T(2,128)}), f32[2,64,256]{2,0,1:T(2,128)S(1)}, u32[]{:S(2)}, u32[]{:S(2)}) %all-to-all-start.1) | async-done | bytes 131104 | tf_op jit(solution)/shard_map/all_to_all | solution.py:65
  68.5 518.4 %while.34 = (s32[]{:T(128)}, f32[256]{0:T(256)S(1)}, f32[256]{0:T(256)S(1)}, f32[128,256]{1,0:T(8,128)S(1)}, f32[128,256]{1,0:T(8,128)S(1)}, /*index=5*/f32[128]...) while((s32[]{:T(128)}, f32[256]{0:T(256)S(1)}, ...), condition=%wide.region_1.2_spmd.clone, body=%wide.region_0.1_spmd.clone.sunk | while | flops 2309 | bytes 12475 | solution.py:31
  71.8 0.7 fusion.44
  75.8 0.7 fusion.44
  79.9 0.7 fusion.44
  83.9 0.7 fusion.44
  88.0 0.7 fusion.44
  92.0 0.7 fusion.44
  96.1 0.7 fusion.44
  100.1 0.7 fusion.44
  104.2 0.7 fusion.44
  108.2 0.7 fusion.44
  112.3 0.7 fusion.44
  116.3 0.7 fusion.44
  120.4 0.7 fusion.44
  124.4 0.7 fusion.44
  128.5 0.7 fusion.44
  586.9 13.3 %while.35 = (s32[]{:T(128)}, f32[256]{0:T(256)S(1)}, f32[128,256]{1,0:T(8,128)S(1)}, f32[128,256]{1,0:T(8,128)S(1)}, f32[128,256]{1,0:T(8,128)S(1)}, /*index=5*/s32[]{:T(128)}, s32[]{:T(128)}, s32[]{:T(128)}) while((s32[]{:T(128)}, f32[256]{0:T(256)S(1)}, f32[128,256]{1,0:T(8,128)S(1)}, f32[128,256]{1,0:T(8,128)S(1)}, ...), condition=%wide.region_3.4_spmd.clone, body=%wide.region_2.3_spmd.clone.sunk | while | flops 772 | bytes 10355 | solution.py:42
  600.3 15.5 %all_to_all.66 = f32[128,1,256]{2,1,0:T(1,128)S(1)} all-to-all(f32[128,1,256]{2,1,0:T(1,128)S(1)} %reshape.30), channel_id=1, replica_groups=mesh['gz'=64,'ha'=16] {'gz'}, dimensions={0} | all-to-all | bytes 262144 | tf_op jit(solution)/shard_map/all_to_all | solution.py:72
  615.8 5.1 fusion.9
  621.7 14.2 %all_to_all.67 = f32[16,1,2048]{2,1,0:T(1,128)S(1)} all-to-all(f32[16,1,2048]{2,1,0:T(1,128)S(1)} %reshape.34), channel_id=1, replica_groups=mesh['gz'=64,'ha'=16] {'ha'}, dimensions={0} | all-to-all | bytes 262144 | tf_op jit(solution)/shard_map/all_to_all | solution.py:78
  635.9 0.9 reduce.1
  637.8 5.7 fusion.7
  (1167 shorter events, 259.0 us)
Async XLA Ops:
  0.0 0.9 copy-start
  7.5 27.4 %all-to-all-start = ((f32[16,1,2048]{2,1,0:T(1,128)}), f32[16,1,2048]{2,1,0:T(1,128)S(1)}, u32[]{:S(2)}, u32[]{:S(2)}) async-start(f32[16,1,2048]{2,1,0:T(1,128)} %reshape.32), calls=%async_computation | async-start | bytes 262144 | tf_op jit(solution)/shard_map/all_to_all | solution.py:56
  43.2 25.2 %all-to-all-start.1 = ((f32[2,64,256]{2,0,1:T(2,128)}), f32[2,64,256]{2,0,1:T(2,128)S(1)}, u32[]{:S(2)}, u32[]{:S(2)}) async-start(f32[2,64,256]{2,0,1:T(2,128)} %copy.9), calls=%async_computation.1 | async-start | bytes 262144 | tf_op jit(solution)/shard_map/all_to_all | solution.py:65
  56.5 0.7 copy-start.1
where the time goes:
time: 649 us; the launch traced here: 643 us
  loops' own time  267 us (41%)
  local copies, waits for them, and re-layouts  185 us (29%)
  other arithmetic  88.3 us (14%)
  starting transfers between devices  31.4 us (5%)
  blocking collectives  29.6 us (5%)
  matrix products  21 us (3%)
  waiting for transfers between devices  20.2 us (3%)
    another operation x1, loops' own time, forward_sweep(): lax.scan(forward, (start_c, start_d), (lower, upper, rhs))  263 us
    dynamic_slice x512, local copies, waits for them, and re-layouts, forward_sweep(): lax.scan(forward, (start_c, start_d), (lower, upper, rhs))  161 us
    div x128, other arithmetic, forward(): dnext = (value + low * dprime) / pivot  84.6 us
    all_to_all x1, starting transfers between devices, on_device(): lax.all_to_all(half, 'ha', split_axis=1, concat_axis=2, tiled=True)  18.2 us
    dynamic_update_slice x384, local copies, waits for them, and re-layouts, forward_sweep(): lax.scan(forward, (start_c, start_d), (lower, upper, rhs))  16.6 us
    all_to_all x1, blocking collectives, on_device(): lax.all_to_all(solved.reshape(depth * slabs, 1, share), 'gz', split_axis=...  15.5 us
    all_to_all x1, blocking collectives, on_device(): grid = lax.all_to_all(back, 'ha', split_axis=2, concat_axis=1, tiled=True)  14.2 us
    all_to_all x1, starting transfers between devices, on_device(): lax.all_to_all(blocks, 'gz', split_axis=1, concat_axis=0, tiled=True)  13.2 us
  transfers between devices with their start and end apart: 2, of which 2 were waited for; matrix products, arithmetic and copies ran while one was open for 0% of the time, Pallas kernels for 0%

commit v1 on v0

v1 whole, which is shorter than its diff:
```python
import math

import jax
import jax.numpy as jnp
import ml_dtypes
import numpy as np
from jax import lax
from jax.experimental import pallas as pl
from jax.experimental.pallas import tpu as pltpu
from jax.sharding import Mesh, PartitionSpec as P

N = 512
M = N // 2
NZ = 128
BY = 8
BX = 8
HA = 16
BLOCK = NZ // BY
F32 = jnp.float32
BF16 = jnp.bfloat16


def tables():
    j = np.arange(M)
    def cas(phase):
        t = 2.0 * np.pi * (phase % N) / N
        return (np.cos(t) + np.sin(t)) / math.sqrt(N)
    even = cas(2 * j[:, None] * j[None, :])
    odd = cas((2 * j[:, None] + 1) * j[None, :])
    def split(a):
        hi = a.astype(ml_dtypes.bfloat16)
        return [hi, (a - hi.astype(np.float64)).astype(ml_dtypes.bfloat16)]
    forward = np.stack(split(even) + split(odd.T))
    inverse = np.stack(split(even) + split(odd))
    eigen = 2.0 - 2.0 * np.cos(2.0 * np.pi * np.arange(N) / N)
    parity = (np.arange(8) // 2) % 2
    eigen_y = eigen[2 * j[None, :] + parity[:, None]]
    return forward, inverse, eigen.astype(np.float32), eigen_y.astype(np.float32)


def product(value, high, low):
    top = value.astype(BF16)
    rest = (value - top.astype(F32)).astype(BF16)
    rows = value.shape[0]
    both = jnp.dot(jnp.concatenate([top, rest], 0), high, preferred_element_type=F32)
    return both[:rows] + both[rows:] + jnp.dot(top, low, preferred_element_type=F32)


def swap_blocks(value):
    sub = lax.broadcasted_iota(jnp.int32, value.shape, 1) // 2
    lane = lax.broadcasted_iota(jnp.int32, value.shape, 2) // 32
    which = (sub - lane) & 3
    out = value
    for s in range(1, 4):
        moved = pltpu.roll(pltpu.roll(value, 2 * s, 1), 128 - 32 * s, 2)
        out = jnp.where(which == s, moved, out)
    return out


def first_of_pair(shape):
    return ((lax.broadcasted_iota(jnp.int32, shape, 1) // 2) & 1) == 0


def forward_x(source, table, out):
    value = source[...]
    left, right = value[:, :M], value[:, M:]
    even = product(left + right, table[0], table[1])
    odd = product(left - right, table[2], table[3])
    out[...] = jnp.concatenate([even, odd], 0).T


def inverse_x(spectral, table, out):
    value = spectral[...].T
    even = product(value[:64], table[0], table[1])
    odd = product(value[64:], table[2], table[3])
    out[:, :M] = even + odd
    out[:, M:] = even - odd


def coefficients(faces, eigen, eigen_y, up_out, down_out, weight_out, ups, downs):
    first = 4 * (lax.axis_index("x") * HA + lax.axis_index("h"))
    sub = lax.broadcasted_iota(jnp.int32, (8, M), 0)
    wave = 2 * (sub & 1) + (sub >> 2)
    shift = eigen_y[...]
    for e in range(4):
        shift = shift + jnp.where(wave == e, eigen[first + e], 0.0)

    def inv(index):
        return 1.0 / jnp.full((8, M), faces[index], F32)

    def steps(i, carry):
        p, u, q, w = carry
        for k in range(8):
            z = i * 8 + k
            p = p + inv(z) * u
            u = u + shift * p
            ups[z] = p
            q = q + inv(NZ - z) * w
            w = w + shift * q
            downs[NZ - 1 - z] = q
        return p, u, q, w

    zero = jnp.zeros((8, M), F32)
    one = jnp.ones((8, M), F32)
    p, u, q, w = lax.fori_loop(0, NZ // 8, steps, (zero, one, zero, one))
    weight_out[...] = 1.0 / (p + inv(NZ) * u)
    base = lax.axis_index("y") * BLOCK
    up_out[...] = ups[pl.ds(base, BLOCK)]
    down_out[...] = downs[pl.ds(base, BLOCK)]


def forward_y(received, table, ups, downs, weight, local, sums):
    value = received[...].reshape(BX, 2, 2, 8, 128)
    low, high = value[:, 0], value[:, 1]

    def lines(part):
        part = swap_blocks(part.reshape(BX * 2, 8, 128)).reshape(BX, 2, 8, 128)
        return jnp.concatenate([part[:, 0].reshape(64, 128), part[:, 1].reshape(64, 128)], 1)

    even = product(lines(low + high), table[0], table[1]).reshape(BX, 8, M)
    odd = product(lines(low - high), table[2], table[3]).reshape(BX, 8, M)
    mask = first_of_pair((BX, 8, M))
    scale = weight[...]
    lower = jnp.where(mask, even, pltpu.roll(odd, 2, 1)) * scale
    upper = jnp.where(mask, pltpu.roll(even, 6, 1), odd) * scale
    rows = [(lower if j % 2 == 0 else upper)[j // 2] for j in range(BLOCK)]
    above = [None] * BLOCK
    total_q = jnp.zeros((8, M), F32)
    for j in reversed(range(BLOCK)):
        above[j] = total_q
        total_q = total_q + downs[j] * rows[j]
    total_p = jnp.zeros((8, M), F32)
    for j in range(BLOCK):
        total_p = total_p + ups[j] * rows[j]
        local[j] = downs[j] * total_p + ups[j] * above[j]
    me = lax.axis_index("y")
    for b in range(BY):
        sums[b] = jnp.where(b > me, total_p, total_q)


def inverse_y(local, ups, downs, sums, table, out):
    me = lax.axis_index("y")
    below = jnp.zeros((8, M), F32)
    above = jnp.zeros((8, M), F32)
    for b in range(BY):
        below = below + jnp.where(b < me, sums[b], 0.0)
        above = above + jnp.where(b > me, sums[b], 0.0)
    value = local[...] + downs[...] * below + ups[...] * above
    value = value.reshape(BX, 2, 8, M)
    lower, upper = value[:, 0], value[:, 1]
    mask = first_of_pair((BX, 8, M))
    even = jnp.where(mask, lower, pltpu.roll(upper, 2, 1)).reshape(64, M)
    odd = jnp.where(mask, pltpu.roll(lower, 6, 1), upper).reshape(64, M)
    even = product(even, table[0], table[1])
    odd = product(odd, table[2], table[3])
    for half, part in enumerate((even + odd, even - odd)):
        for side in range(2):
            piece = part[:, side * 128 : (side + 1) * 128].reshape(BX, 8, 128)
            out[:, half, side] = swap_blocks(piece)


def shape(*dims):
    return jax.ShapeDtypeStruct(dims, F32)


VMEM = pl.BlockSpec(memory_space=pltpu.VMEM)
SMEM = pl.BlockSpec(memory_space=pltpu.SMEM)


def on_device(source, faces):
    forward, inverse, eigen, eigen_y = (jnp.asarray(t) for t in tables())
    with jax.named_scope("coefficients"):
        ups, downs, weight = pl.pallas_call(
            coefficients,
            out_shape=(shape(BLOCK, 8, M), shape(BLOCK, 8, M), shape(8, M)),
            in_specs=[SMEM, SMEM, VMEM],
            out_specs=(VMEM, VMEM, VMEM),
            scratch_shapes=[pltpu.VMEM((NZ, 8, M), F32), pltpu.VMEM((NZ, 8, M), F32)],
        )(faces, eigen, eigen_y)
    with jax.named_scope("forward_x"):
        half = pl.pallas_call(
            forward_x, out_shape=shape(M, 128), in_specs=[VMEM, VMEM], out_specs=VMEM
        )(source.reshape(64, N), forward)
    with jax.named_scope("exchange_out"):
        pencils = lax.all_to_all(half.reshape(BX * HA, 2, 128), ("x", "h"), 0, 0, tiled=True)
    with jax.named_scope("forward_y"):
        local, sums = pl.pallas_call(
            forward_y,
            out_shape=(shape(BLOCK, 8, M), shape(BY, 8, M)),
            in_specs=[VMEM] * 5,
            out_specs=(VMEM, VMEM),
        )(pencils.reshape(M, 128), forward, ups, downs, weight)
    with jax.named_scope("exchange_sums"):
        sums = lax.all_to_all(sums, "y", 0, 0, tiled=True)
    with jax.named_scope("inverse_y"):
        back = pl.pallas_call(
            inverse_y,
            out_shape=shape(BX, 2, 2, 8, 128),
            in_specs=[VMEM] * 5,
            out_specs=VMEM,
        )(local, ups, downs, sums, inverse)
    with jax.named_scope("exchange_back"):
        grid = lax.all_to_all(back.reshape(BX * HA, 2, 128), ("x", "h"), 0, 0, tiled=True)
    with jax.named_scope("inverse_x"):
        out = pl.pallas_call(
            inverse_x, out_shape=shape(64, N), in_specs=[VMEM, VMEM], out_specs=VMEM
        )(grid.reshape(M, 128), inverse)
    return out.reshape(2, 32, N)


def solution(mesh):
    fine = Mesh(mesh.devices.reshape(BY, BX, HA), ("y", "x", "h"))
    return jax.shard_map(
        on_device,
        mesh=fine,
        in_specs=(P(("y", "x"), "h", None), P()),
        out_specs=P(("y", "x"), "h", None),
        check_vma=False,
    )
```

time: 649 us -> 82 us (0.13)
  loops' own time: 267 us -> 0 us
  local copies, waits for them, and re-layouts: 185 us -> 0.65 us
  other arithmetic: 88.3 us -> 0 us
  matrix products: 21 us -> 0 us
  Pallas kernels: 0 us -> 10.8 us
  waiting for transfers between devices: 20.2 us -> 9.98 us
  starting transfers between devices: 31.4 us -> 24.4 us
    another operation x2 -> x0, loops' own time: 267 us -> none  [the longest x1 263 us: forward_sweep(): lax.scan(forward, (start_c, start_d), (lower, upper, rhs))]
    dynamic_slice x513 -> x0, local copies, waits for them, and re-layouts: 161 us -> none  [the longest x512 161 us: forward_sweep(): lax.scan(forward, (start_c, start_d), (lower, upper, rhs))]
    div x128 -> x0, other arithmetic: 84.6 us -> none  [forward(): dnext = (value + low * dprime) / pivot]
    dot_general x4 -> x0, matrix products: 21 us -> none  [the longest x1 5.67 us: on_device(): return jnp.einsum('zky,kx->zyx', grid, hx, precision=HIGH)]
    dynamic_update_slice x384 -> x0, local copies, waits for them, and re-layouts: 16.6 us -> none  [forward_sweep(): lax.scan(forward, (start_c, start_d), (lower, upper, rhs))]
    pallas_call x0 -> x5, Pallas kernels: none -> 10.8 us  [the longest x1 2.32 us: on_device(): pl.pallas_call(inverse_y, out_shape=shape(BX, 2, 2, 8, 128), in_specs=[VM...]
    all_to_all x2 -> x1, waiting for transfers between devices: 20.2 us -> 9.98 us  [on_device(): lax.all_to_all(half.reshape(BX * HA, 2, 128), ('x', 'h'), 0, 0, tiled=True)]
    all_to_all x2 -> x1, starting transfers between devices: 31.4 us -> 24.4 us  [on_device(): lax.all_to_all(half.reshape(BX * HA, 2, 128), ('x', 'h'), 0, 0, tiled=True)]
  transfers between devices with their start and end apart: 2 -> 1, of which waited for: 2 -> 1; matrix products, arithmetic and copies ran while one was open for 0% -> 0% of each run, Pallas kernels for 0% -> 3%
where the time goes in v1:
time: 82 us; the launch traced here: 81.6 us
  blocking collectives  35.6 us (43%)
  starting transfers between devices  24.4 us (30%)
  Pallas kernels  10.8 us (13%)
  waiting for transfers between devices  9.98 us (12%)
    all_to_all x1, starting transfers between devices, on_device(): lax.all_to_all(half.reshape(BX * HA, 2, 128), ('x', 'h'), 0, 0, tiled=True)  24.4 us
    all_to_all x1, blocking collectives, on_device(): lax.all_to_all(back.reshape(BX * HA, 2, 128), ('x', 'h'), 0, 0, tiled=True)  21 us
    all_to_all x1, blocking collectives, on_device(): sums = lax.all_to_all(sums, 'y', 0, 0, tiled=True)  14.6 us
    all_to_all x1, waiting for transfers between devices, on_device(): lax.all_to_all(half.reshape(BX * HA, 2, 128), ('x', 'h'), 0, 0, tiled=True)  9.98 us
    pallas_call x1, Pallas kernels, on_device(): pl.pallas_call(inverse_y, out_shape=shape(BX, 2, 2, 8, 128), in_specs=[VM...  2.32 us
    pallas_call x1, Pallas kernels, on_device(): pl.pallas_call(coefficients, out_shape=(shape(BLOCK, 8, M), shape(BLOCK,...  2.22 us
    pallas_call x1, Pallas kernels, on_device(): pl.pallas_call(forward_y, out_shape=(shape(BLOCK, 8, M), shape(BY, 8, M))...  2.19 us
    pallas_call x1, Pallas kernels, on_device(): pl.pallas_call(forward_x, out_shape=shape(M, 128), in_specs=[VMEM, VMEM],...  2.07 us
  transfers between devices with their start and end apart: 1, of which 1 were waited for; matrix products, arithmetic and copies ran while one was open for 0% of the time, Pallas kernels for 3%

profile of v1, /device:TPU:1, one launch (start us, length us, event | category | flops | bytes accessed | tf_op | source)
XLA Modules:
  0.0 81.6 jit_solution(6976903927772595875)
XLA Ops:
  0.0 2.1 %forward_x.1 = f32[256,128]{1,0:T(8,128)} custom-call(f32[64,512]{1,0:T(8,128)} %bitcast.10, bf16[4,256,256]{2,1,0:T(8,128)(2,1)} %constant.8.clone.table), custom_call_target="tpu_custom_call" | custom-call | tf_op jit(solution)/shard_map/forward_x/pallas_call | solution.py:181
  2.1 24.4 %all-to-all-start = ((f32[128,2,128]{2,1,0:T(2,128)}), f32[128,2,128]{2,1,0:T(2,128)S(1)}, u32[]{:S(2)}, u32[]{:S(2)}) async-start(f32[128,2,128]{2,1,0:T(2,128)} %bitcast.8), calls=%async_computation | async-start | bytes 262144 | tf_op jit(solution)/shard_map/exchange_out/all_to_all | solution.py:185
  26.5 2.2 %coefficients.1 = (f32[16,8,256]{2,1,0:T(8,128)}, f32[16,8,256]{2,1,0:T(8,128)}, f32[8,256]{1,0:T(8,128)}) custom-call(f32[129]{0:T(256)} %faces.1, f32[512]{0:T(512)} %constant.10.clone.eigen, f32[8,256]{1,0:T(8,128)} %constant.11.clone.eigen_y), custom_call_target="tpu_custom_call" | custom-call | tf_op jit(solution)/shard_map/coefficients/pallas_call | solution.py:173
  28.7 10.0 %all-to-all-done = f32[128,2,128]{2,1,0:T(2,128)S(1)} async-done(((f32[128,2,128]{2,1,0:T(2,128)}), f32[128,2,128]{2,1,0:T(2,128)S(1)}, u32[]{:S(2)}, u32[]{:S(2)}) %all-to-all-start) | async-done | bytes 131104 | tf_op jit(solution)/shard_map/exchange_out/all_to_all | solution.py:185
  38.7 0.0 copy-start
  38.7 0.7 copy-done
  39.4 2.2 %forward_y.1 = (f32[16,8,256]{2,1,0:T(8,128)}, f32[8,8,256]{2,1,0:T(8,128)}) custom-call(f32[256,128]{1,0:T(8,128)} %bitcast.6, bf16[4,256,256]{2,1,0:T(8,128)(2,1)} %constant.8.clone.table, f32[16,8,256]{2,1,0:T(8,128)} %get-tuple-element.10.ups, f32[16,8,256]{2,1,0:T(8,128)} %get-tuple-element.11.downs, f32[8,256]{1,0:T(8,128)} %get-tuple-element.12.weight), custom_call_target="tpu_custom_call" | custom-call | tf_op jit(solution)/shard_map/forward_y/pallas_call | solution.py:187
  41.6 14.6 %all_to_all.15.sums = f32[8,8,256]{2,1,0:T(8,128)} all-to-all(f32[8,8,256]{2,1,0:T(8,128)} %get-tuple-element.14), channel_id=1, replica_groups=mesh['y'=8,'x'=8,'h'=16] {'y'}, dimensions={0} | all-to-all | bytes 131072 | tf_op jit(solution)/shard_map/exchange_sums/all_to_all | solution.py:194
  56.2 2.3 %inverse_y.1 = f32[8,2,2,8,128]{4,3,2,1,0:T(8,128)} custom-call(f32[16,8,256]{2,1,0:T(8,128)} %get-tuple-element.13.local, f32[16,8,256]{2,1,0:T(8,128)} %get-tuple-element.10.ups, f32[16,8,256]{2,1,0:T(8,128)} %get-tuple-element.11.downs, f32[8,8,256]{2,1,0:T(8,128)} %all_to_all.15.sums, bf16[4,256,256]{2,1,0:T(8,128)(2,1)} %constant.9.clone.table), custom_call_target="tpu_custom_call" | custom-call | tf_op jit(solution)/shard_map/inverse_y/pallas_call | solution.py:196
  58.5 21.0 %all_to_all.16 = f32[128,2,128]{2,1,0:T(2,128)} all-to-all(f32[128,2,128]{2,1,0:T(2,128)} %bitcast.7), channel_id=1, replica_groups=mesh['y'=8,'x'=8,'h'=16] {'x','h'}, dimensions={0} | all-to-all | bytes 262144 | tf_op jit(solution)/shard_map/exchange_back/all_to_all | solution.py:203
  79.5 2.0 %inverse_x.1 = f32[64,512]{1,0:T(8,128)} custom-call(f32[256,128]{1,0:T(8,128)} %bitcast.9, bf16[4,256,256]{2,1,0:T(8,128)(2,1)} %constant.9.clone.table), custom_call_target="tpu_custom_call" | custom-call | tf_op jit(solution)/shard_map/inverse_x/pallas_call | solution.py:205
Async XLA Ops:
  2.1 36.7 %all-to-all-start = ((f32[128,2,128]{2,1,0:T(2,128)}), f32[128,2,128]{2,1,0:T(2,128)S(1)}, u32[]{:S(2)}, u32[]{:S(2)}) async-start(f32[128,2,128]{2,1,0:T(2,128)} %bitcast.8), calls=%async_computation | async-start | bytes 262144 | tf_op jit(solution)/shard_map/exchange_out/all_to_all | solution.py:185
  38.7 0.7 copy-start

commit v2 on v1

--- a/solution.py
+++ b/solution.py
@@ -164,6 +164,7 @@
 
 
 VMEM = pl.BlockSpec(memory_space=pltpu.VMEM)
+SMALL = pltpu.CompilerParams(vmem_limit_bytes=8 * 1024 * 1024)
 SMEM = pl.BlockSpec(memory_space=pltpu.SMEM)
 
 
@@ -176,10 +177,15 @@
             in_specs=[SMEM, SMEM, VMEM],
             out_specs=(VMEM, VMEM, VMEM),
             scratch_shapes=[pltpu.VMEM((NZ, 8, M), F32), pltpu.VMEM((NZ, 8, M), F32)],
+            compiler_params=SMALL,
         )(faces, eigen, eigen_y)
     with jax.named_scope("forward_x"):
         half = pl.pallas_call(
-            forward_x, out_shape=shape(M, 128), in_specs=[VMEM, VMEM], out_specs=VMEM
+            forward_x,
+            out_shape=shape(M, 128),
+            in_specs=[VMEM, VMEM],
+            out_specs=VMEM,
+            compiler_params=SMALL,
         )(source.reshape(64, N), forward)
     with jax.named_scope("exchange_out"):
         pencils = lax.all_to_all(half.reshape(BX * HA, 2, 128), ("x", "h"), 0, 0, tiled=True)
@@ -189,6 +195,7 @@
             out_shape=(shape(BLOCK, 8, M), shape(BY, 8, M)),
             in_specs=[VMEM] * 5,
             out_specs=(VMEM, VMEM),
+            compiler_params=SMALL,
         )(pencils.reshape(M, 128), forward, ups, downs, weight)
     with jax.named_scope("exchange_sums"):
         sums = lax.all_to_all(sums, "y", 0, 0, tiled=True)
@@ -198,12 +205,17 @@
             out_shape=shape(BX, 2, 2, 8, 128),
             in_specs=[VMEM] * 5,
             out_specs=VMEM,
+            compiler_params=SMALL,
         )(local, ups, downs, sums, inverse)
     with jax.named_scope("exchange_back"):
         grid = lax.all_to_all(back.reshape(BX * HA, 2, 128), ("x", "h"), 0, 0, tiled=True)
     with jax.named_scope("inverse_x"):
         out = pl.pallas_call(
-            inverse_x, out_shape=shape(64, N), in_specs=[VMEM, VMEM], out_specs=VMEM
+            inverse_x,
+            out_shape=shape(64, N),
+            in_specs=[VMEM, VMEM],
+            out_specs=VMEM,
+            compiler_params=SMALL,
         )(grid.reshape(M, 128), inverse)
     return out.reshape(2, 32, N)
 

time: 82 us -> 75.6 us (0.922)
  Pallas kernels: 10.8 us -> 4.03 us
  blocking collectives: 35.6 us -> 33.9 us
  local copies, waits for them, and re-layouts: 0.65 us -> 1.96 us
  waiting for transfers between devices: 9.98 us -> 10.8 us
    pallas_call x1, Pallas kernels: 2.32 us -> 0.41 us  [on_device(): pl.pallas_call(inverse_y, out_shape=shape(BX, 2, 2, 8, 128), in_specs=[VM...]
    pallas_call x1, Pallas kernels: 2.19 us -> 0.36 us  [on_device(): pl.pallas_call(forward_y, out_shape=(shape(BLOCK, 8, M), shape(BY, 8, M))...]
    all_to_all x1, blocking collectives: 21 us -> 19.6 us  [on_device(): lax.all_to_all(back.reshape(BX * HA, 2, 128), ('x', 'h'), 0, 0, tiled=True)]
    unnamed x2 -> x14, local copies, waits for them, and re-layouts: 0.65 us -> 1.96 us
    pallas_call x1, Pallas kernels: 2.07 us -> 0.95 us  [on_device(): pl.pallas_call(forward_x, out_shape=shape(M, 128), in_specs=[VMEM, VMEM],...]
    pallas_call x1, Pallas kernels: 2.04 us -> 0.93 us  [on_device(): pl.pallas_call(inverse_x, out_shape=shape(64, N), in_specs=[VMEM, VMEM],...]
    pallas_call x1, Pallas kernels: 2.22 us -> 1.37 us  [on_device(): pl.pallas_call(coefficients, out_shape=(shape(BLOCK, 8, M), shape(BLOCK,...]
  transfers between devices with their start and end apart: 1 -> 1, of which waited for: 1 -> 1; matrix products, arithmetic and copies ran while one was open for 0% -> 0% of each run, Pallas kernels for 3% -> 2%
where the time goes in v2:
time: 75.6 us; the launch traced here: 75.3 us
  blocking collectives  33.9 us (45%)
  starting transfers between devices  24.6 us (33%)
  waiting for transfers between devices  10.8 us (14%)
  Pallas kernels  4.03 us (5%)
  local copies, waits for them, and re-layouts  1.96 us (3%)
    all_to_all x1, starting transfers between devices, on_device(): lax.all_to_all(half.reshape(BX * HA, 2, 128), ('x', 'h'), 0, 0, tiled=True)  24.6 us
    all_to_all x1, blocking collectives, on_device(): lax.all_to_all(back.reshape(BX * HA, 2, 128), ('x', 'h'), 0, 0, tiled=True)  19.6 us
    all_to_all x1, blocking collectives, on_device(): sums = lax.all_to_all(sums, 'y', 0, 0, tiled=True)  14.3 us
    all_to_all x1, waiting for transfers between devices, on_device(): lax.all_to_all(half.reshape(BX * HA, 2, 128), ('x', 'h'), 0, 0, tiled=True)  10.8 us
    unnamed x14, local copies, waits for them, and re-layouts  1.96 us
  transfers between devices with their start and end apart: 1, of which 1 were waited for; matrix products, arithmetic and copies ran while one was open for 0% of the time, Pallas kernels for 2%

profile of v2, /device:TPU:1, one launch (start us, length us, event | category | flops | bytes accessed | tf_op | source)
XLA Modules:
  0.0 75.3 jit_solution(13651790509872341938)
XLA Ops:
  0.0 0.0 copy-start
  0.0 1.0 %copy-done = bf16[4,256,256]{2,1,0:T(8,128)(2,1)S(1)} copy-done((bf16[4,256,256]{2,1,0:T(8,128)(2,1)S(1)}, bf16[4,256,256]{2,1,0:T(8,128)(2,1)}, u32[]{:S(2)}) %copy-start) | copy-done | bytes 524312
  1.0 0.0 copy-start.3
  1.0 0.9 %copy-done.3 = f32[2,32,512]{2,1,0:T(8,128)S(1)} copy-done((f32[2,32,512]{2,1,0:T(8,128)S(1)}, f32[2,32,512]{2,1,0:T(8,128)}, u32[]{:S(2)}) %copy-start.3) | copy-done | bytes 131096
  1.9 0.0 copy-start.1
  1.9 1.0 %forward_x.1 = f32[256,128]{1,0:T(8,128)} custom-call(f32[64,512]{1,0:T(8,128)S(1)} %bitcast.9, bf16[4,256,256]{2,1,0:T(8,128)(2,1)S(1)} %copy-done), custom_call_target="tpu_custom_call" | custom-call | tf_op jit(solution)/shard_map/forward_x/pallas_call | solution.py:183
  2.9 0.0 copy-start.4
  2.9 0.0 copy-start.5
  2.9 0.0 copy-start.6
  2.9 24.6 %all-to-all-start = ((f32[128,2,128]{2,1,0:T(2,128)}), f32[128,2,128]{2,1,0:T(2,128)S(1)}, u32[]{:S(2)}, u32[]{:S(2)}) async-start(f32[128,2,128]{2,1,0:T(2,128)} %bitcast.1), calls=%async_computation | async-start | bytes 262144 | tf_op jit(solution)/shard_map/exchange_out/all_to_all | solution.py:191
  27.5 0.0 copy-done.4
  27.5 0.0 copy-done.5
  27.5 0.0 copy-done.6
  27.5 1.4 %coefficients.1 = (f32[16,8,256]{2,1,0:T(8,128)S(1)}, f32[16,8,256]{2,1,0:T(8,128)S(1)}, f32[8,256]{1,0:T(8,128)S(1)}) custom-call(f32[129]{0:T(256)S(1)} %copy-done.6, f32[512]{0:T(512)S(1)} %copy-done.5, f32[8,256]{1,0:T(8,128)S(1)} %copy-done.4), custom_call_target="tpu_custom_call" | custom-call | tf_op jit(solution)/shard_map/coefficients/pallas_call | solution.py:174
  28.9 10.8 %all-to-all-done = f32[128,2,128]{2,1,0:T(2,128)S(1)} async-done(((f32[128,2,128]{2,1,0:T(2,128)}), f32[128,2,128]{2,1,0:T(2,128)S(1)}, u32[]{:S(2)}, u32[]{:S(2)}) %all-to-all-start) | async-done | bytes 131104 | tf_op jit(solution)/shard_map/exchange_out/all_to_all | solution.py:191
  39.7 0.0 copy-done.1
  39.7 0.0 copy-start.2
  39.7 0.4 forward_y.1
  40.1 14.3 %all_to_all.15.sums = f32[8,8,256]{2,1,0:T(8,128)S(1)} all-to-all(f32[8,8,256]{2,1,0:T(8,128)S(1)} %get-tuple-element.14), channel_id=1, replica_groups=mesh['y'=8,'x'=8,'h'=16] {'y'}, dimensions={0} | all-to-all | bytes 131072 | tf_op jit(solution)/shard_map/exchange_sums/all_to_all | solution.py:201
  54.4 0.0 copy-done.2
  54.4 0.4 inverse_y.1
  54.8 19.6 %all_to_all.16 = f32[128,2,128]{2,1,0:T(2,128)S(1)} all-to-all(f32[128,2,128]{2,1,0:T(2,128)S(1)} %bitcast.7), channel_id=1, replica_groups=mesh['y'=8,'x'=8,'h'=16] {'x','h'}, dimensions={0} | all-to-all | bytes 262144 | tf_op jit(solution)/shard_map/exchange_back/all_to_all | solution.py:211
  74.4 0.9 %inverse_x.1 = f32[64,512]{1,0:T(8,128)} custom-call(f32[256,128]{1,0:T(8,128)S(1)} %bitcast.8, bf16[4,256,256]{2,1,0:T(8,128)(2,1)S(1)} %copy-done.2), custom_call_target="tpu_custom_call" | custom-call | tf_op jit(solution)/shard_map/inverse_x/pallas_call | solution.py:213
Async XLA Ops:
  0.0 1.0 %copy-start = (bf16[4,256,256]{2,1,0:T(8,128)(2,1)S(1)}, bf16[4,256,256]{2,1,0:T(8,128)(2,1)}, u32[]{:S(2)}) copy-start(bf16[4,256,256]{2,1,0:T(8,128)(2,1)} %constant.8.clone.table) | copy-start | bytes 1572868
  1.0 0.9 %copy-start.3 = (f32[2,32,512]{2,1,0:T(8,128)S(1)}, f32[2,32,512]{2,1,0:T(8,128)}, u32[]{:S(2)}) copy-start(f32[2,32,512]{2,1,0:T(8,128)} %param.6) | copy-start | bytes 393220
  1.9 37.8 %copy-start.1 = (bf16[4,256,256]{2,1,0:T(8,128)(2,1)S(1)}, bf16[4,256,256]{2,1,0:T(8,128)(2,1)}, u32[]{:S(2)}) copy-start(bf16[4,256,256]{2,1,0:T(8,128)(2,1)} %constant.8.clone.table) | copy-start | bytes 1572868
  2.9 24.6 %copy-start.4 = (f32[8,256]{1,0:T(8,128)S(1)}, f32[8,256]{1,0:T(8,128)}, u32[]{:S(2)}) copy-start(f32[8,256]{1,0:T(8,128)} %constant.11.clone.eigen_y) | copy-start | bytes 24580
  2.9 24.6 %copy-start.5 = (f32[512]{0:T(512)S(1)}, f32[512]{0:T(512)}, u32[]{:S(2)}) copy-start(f32[512]{0:T(512)} %constant.10.clone.eigen) | copy-start | bytes 6148
  2.9 24.6 %copy-start.6 = (f32[129]{0:T(256)S(1)}, f32[129]{0:T(256)}, u32[]{:S(2)}) copy-start(f32[129]{0:T(256)} %faces.1) | copy-start | bytes 1552
  2.9 36.8 %all-to-all-start = ((f32[128,2,128]{2,1,0:T(2,128)}), f32[128,2,128]{2,1,0:T(2,128)S(1)}, u32[]{:S(2)}, u32[]{:S(2)}) async-start(f32[128,2,128]{2,1,0:T(2,128)} %bitcast.1), calls=%async_computation | async-start | bytes 262144 | tf_op jit(solution)/shard_map/exchange_out/all_to_all | solution.py:191
  39.7 14.7 %copy-start.2 = (bf16[4,256,256]{2,1,0:T(8,128)(2,1)S(1)}, bf16[4,256,256]{2,1,0:T(8,128)(2,1)}, u32[]{:S(2)}) copy-start(bf16[4,256,256]{2,1,0:T(8,128)(2,1)} %constant.9.clone.table) | copy-start | bytes 1572868

commit v3 on v2

--- a/solution.py
+++ b/solution.py
@@ -61,12 +61,29 @@
     return ((lax.broadcasted_iota(jnp.int32, shape, 1) // 2) & 1) == 0
 
 
-def forward_x(source, table, out):
-    value = source[...]
+def first_kernel(
+    source, table, faces, eigen, eigen_y, half, up_out, down_out, weight_out,
+    value, matrix, face, wave, wave_y, below_p, below_u, above_q, above_w, sems,
+):
+    copies = [
+        pltpu.make_async_copy(src, dst, sems.at[n])
+        for n, (src, dst) in enumerate(
+            ((faces, face), (eigen, wave), (eigen_y, wave_y), (source, value), (table, matrix))
+        )
+    ]
+    for copy in copies:
+        copy.start()
+    for copy in copies[:3]:
+        copy.wait()
+    coefficients(
+        face, wave, wave_y, up_out, down_out, weight_out, below_p, below_u, above_q, above_w
+    )
+    for copy in copies[3:]:
+        copy.wait()
     left, right = value[:, :M], value[:, M:]
-    even = product(left + right, table[0], table[1])
-    odd = product(left - right, table[2], table[3])
-    out[...] = jnp.concatenate([even, odd], 0).T
+    even = product(left + right, matrix[0], matrix[1])
+    odd = product(left - right, matrix[2], matrix[3])
+    half[...] = jnp.concatenate([even, odd], 0).T
 
 
 def inverse_x(spectral, table, out):
@@ -77,7 +94,7 @@
     out[:, M:] = even - odd
 
 
-def coefficients(faces, eigen, eigen_y, up_out, down_out, weight_out, ups, downs):
+def coefficients(faces, eigen, eigen_y, up_out, down_out, weight_out, ps, us, qs, ws):
     first = 4 * (lax.axis_index("x") * HA + lax.axis_index("h"))
     sub = lax.broadcasted_iota(jnp.int32, (8, M), 0)
     wave = 2 * (sub & 1) + (sub >> 2)
@@ -86,27 +103,46 @@
         shift = shift + jnp.where(wave == e, eigen[first + e], 0.0)
 
     def inv(index):
-        return 1.0 / jnp.full((8, M), faces[index], F32)
-
-    def steps(i, carry):
-        p, u, q, w = carry
-        for k in range(8):
-            z = i * 8 + k
-            p = p + inv(z) * u
-            u = u + shift * p
-            ups[z] = p
-            q = q + inv(NZ - z) * w
-            w = w + shift * q
-            downs[NZ - 1 - z] = q
-        return p, u, q, w
-
-    zero = jnp.zeros((8, M), F32)
-    one = jnp.ones((8, M), F32)
-    p, u, q, w = lax.fori_loop(0, NZ // 8, steps, (zero, one, zero, one))
-    weight_out[...] = 1.0 / (p + inv(NZ) * u)
-    base = lax.axis_index("y") * BLOCK
-    up_out[...] = ups[pl.ds(base, BLOCK)]
-    down_out[...] = downs[pl.ds(base, BLOCK)]
+        half = 1.0 / jnp.full((8, 128), faces[index], F32)
+        return jnp.concatenate([half, half], 1)
+
+    blocks = []
+    for b in range(BY):
+        g = inv(b * BLOCK)
+        pa, ua = jnp.ones((8, M), F32), shift
+        pb, ub = g, 1.0 + shift * g
+        for j in range(1, BLOCK):
+            g = inv(b * BLOCK + j)
+            pa = pa + g * ua
+            ua = ua + shift * pa
+            pb = pb + g * ub
+            ub = ub + shift * pb
+        blocks.append((pa, pb, ua, ub))
+    p, u = jnp.zeros((8, M), F32), jnp.ones((8, M), F32)
+    for b in range(BY):
+        ps[b], us[b] = p, u
+        pa, pb, ua, ub = blocks[b]
+        p, u = pa * p + pb * u, ua * p + ub * u
+    last = inv(NZ)
+    weight_out[...] = 1.0 / (p + last * u)
+    q, w = last, jnp.ones((8, M), F32)
+    for b in reversed(range(BY)):
+        qs[b], ws[b] = q, w
+        pa, pb, ua, ub = blocks[b]
+        q, w = ub * q + pb * w, ua * q + pa * w
+
+    me = lax.axis_index("y")
+    inner = [inv(me * BLOCK + j) for j in range(BLOCK)]
+    p, u = ps[me], us[me]
+    q, w = qs[me], ws[me]
+    for j in range(BLOCK):
+        p = p + inner[j] * u
+        up_out[j] = p
+        u = u + shift * p
+        k = BLOCK - 1 - j
+        down_out[k] = q
+        w = w + shift * q
+        q = q + inner[k] * w
 
 
 def forward_y(received, table, ups, downs, weight, local, sums):
@@ -165,28 +201,31 @@
 
 VMEM = pl.BlockSpec(memory_space=pltpu.VMEM)
 SMALL = pltpu.CompilerParams(vmem_limit_bytes=8 * 1024 * 1024)
-SMEM = pl.BlockSpec(memory_space=pltpu.SMEM)
+HBM = pl.BlockSpec(memory_space=pltpu.HBM)
 
 
 def on_device(source, faces):
     forward, inverse, eigen, eigen_y = (jnp.asarray(t) for t in tables())
-    with jax.named_scope("coefficients"):
-        ups, downs, weight = pl.pallas_call(
-            coefficients,
-            out_shape=(shape(BLOCK, 8, M), shape(BLOCK, 8, M), shape(8, M)),
-            in_specs=[SMEM, SMEM, VMEM],
-            out_specs=(VMEM, VMEM, VMEM),
-            scratch_shapes=[pltpu.VMEM((NZ, 8, M), F32), pltpu.VMEM((NZ, 8, M), F32)],
-            compiler_params=SMALL,
-        )(faces, eigen, eigen_y)
     with jax.named_scope("forward_x"):
-        half = pl.pallas_call(
-            forward_x,
-            out_shape=shape(M, 128),
-            in_specs=[VMEM, VMEM],
-            out_specs=VMEM,
-            compiler_params=SMALL,
-        )(source.reshape(64, N), forward)
+        half, ups, downs, weight = pl.pallas_call(
+            first_kernel,
+            out_shape=(shape(M, 128), shape(BLOCK, 8, M), shape(BLOCK, 8, M), shape(8, M)),
+            in_specs=[HBM] * 5,
+            out_specs=(VMEM,) * 4,
+            scratch_shapes=[
+                pltpu.VMEM((64, N), F32),
+                pltpu.VMEM((4, M, M), BF16),
+                pltpu.SMEM((NZ + 1,), F32),
+                pltpu.SMEM((N,), F32),
+                pltpu.VMEM((8, M), F32),
+                pltpu.VMEM((BY, 8, M), F32),
+                pltpu.VMEM((BY, 8, M), F32),
+                pltpu.VMEM((BY, 8, M), F32),
+                pltpu.VMEM((BY, 8, M), F32),
+                pltpu.SemaphoreType.DMA((5,)),
+            ],
+            compiler_params=SMALL,
+        )(source.reshape(64, N), forward, faces, eigen, eigen_y)
     with jax.named_scope("exchange_out"):
         pencils = lax.all_to_all(half.reshape(BX * HA, 2, 128), ("x", "h"), 0, 0, tiled=True)
     with jax.named_scope("forward_y"):

time: 75.6 us -> 77.1 us (1.020)
  blocking collectives: 33.9 us -> 70.3 us
  starting transfers between devices: 24.6 us -> 0 us
  waiting for transfers between devices: 10.8 us -> 0 us
  local copies, waits for them, and re-layouts: 1.96 us -> 3.34 us
  Pallas kernels: 4.03 us -> 3.01 us
    all_to_all x0 -> x1, blocking collectives: none -> 36.7 us  [on_device(): lax.all_to_all(half.reshape(BX * HA, 2, 128), ('x', 'h'), 0, 0, tiled=True)]
    all_to_all x1 -> x0, starting transfers between devices: 24.6 us -> none  [on_device(): lax.all_to_all(half.reshape(BX * HA, 2, 128), ('x', 'h'), 0, 0, tiled=True)]
    all_to_all x1 -> x0, waiting for transfers between devices: 10.8 us -> none  [on_device(): lax.all_to_all(half.reshape(BX * HA, 2, 128), ('x', 'h'), 0, 0, tiled=True)]
    unnamed x14, local copies, waits for them, and re-layouts: 1.96 us -> 3.34 us
    pallas_call x2 -> x1, Pallas kernels: 2.33 us -> 1.34 us  [on_device(): pl.pallas_call(first_kernel, out_shape=(shape(M, 128), shape(BLOCK, 8, M)...]
  transfers between devices with their start and end apart: 1 -> 0, of which waited for: 1 -> 0; matrix products, arithmetic and copies ran while one was open for 0% -> 0% of each run, Pallas kernels for 2% -> 0%
where the time goes in v3:
time: 77.1 us; the launch traced here: 76.7 us
  blocking collectives  70.3 us (91%)
  local copies, waits for them, and re-layouts  3.34 us (4%)
  Pallas kernels  3.01 us (4%)
    all_to_all x1, blocking collectives, on_device(): lax.all_to_all(half.reshape(BX * HA, 2, 128), ('x', 'h'), 0, 0, tiled=True)  36.7 us
    all_to_all x1, blocking collectives, on_device(): lax.all_to_all(back.reshape(BX * HA, 2, 128), ('x', 'h'), 0, 0, tiled=True)  19.2 us
    all_to_all x1, blocking collectives, on_device(): sums = lax.all_to_all(sums, 'y', 0, 0, tiled=True)  14.4 us
    unnamed x14, local copies, waits for them, and re-layouts  3.34 us

profile of v3, /device:TPU:1, one launch (start us, length us, event | category | flops | bytes accessed | tf_op | source)
XLA Modules:
  0.0 76.7 jit_solution(4275290170413352340)
XLA Ops:
  0.0 0.0 copy-start.5
  0.0 0.0 copy-start.6
  0.0 0.7 copy-done.5
  0.7 0.0 copy-done.6
  0.7 0.0 copy-start
  0.7 1.0 %copy-done = bf16[4,256,256]{2,1,0:T(8,128)(2,1)S(1)} copy-done((bf16[4,256,256]{2,1,0:T(8,128)(2,1)S(1)}, bf16[4,256,256]{2,1,0:T(8,128)(2,1)}, u32[]{:S(2)}) %copy-start) | copy-done | bytes 524312
  1.7 0.0 copy-start.3
  1.7 0.9 %copy-done.3 = f32[2,32,512]{2,1,0:T(8,128)S(1)} copy-done((f32[2,32,512]{2,1,0:T(8,128)S(1)}, f32[2,32,512]{2,1,0:T(8,128)}, u32[]{:S(2)}) %copy-start.3) | copy-done | bytes 131096
  2.6 0.0 copy-start.4
  2.6 0.7 copy-done.4
  3.3 0.0 copy-start.1
  3.3 1.3 %forward_x.1 = (f32[256,128]{1,0:T(8,128)S(1)}, f32[16,8,256]{2,1,0:T(8,128)S(1)}, f32[16,8,256]{2,1,0:T(8,128)S(1)}, f32[8,256]{1,0:T(8,128)S(1)}) custom-call(f32[64,512]{1,0:T(8,128)S(1)} %bitcast.10, bf16[4,256,256]{2,1,0:T(8,128)(2,1)S(1)} %copy-done, f32[129]{0:T(256)S(1)} %copy-done.6, f32[512]{0:T(512)S(1)} %copy-done.5, f32[8,256]{1,0:T(8,128)S(1)} %copy-done.4), custom_call_target="tpu_custom_call" | custom-call | tf_op jit(solution)/shard_map/forward_x/pallas_call | solution.py:210
  4.7 36.7 %all_to_all.15 = f32[128,2,128]{2,1,0:T(2,128)S(1)} all-to-all(f32[128,2,128]{2,1,0:T(2,128)S(1)} %bitcast.9), channel_id=1, replica_groups=mesh['y'=8,'x'=8,'h'=16] {'x','h'}, dimensions={0} | all-to-all | bytes 262144 | tf_op jit(solution)/shard_map/exchange_out/all_to_all | solution.py:230
  41.4 0.0 copy-done.1
  41.4 0.0 copy-start.2
  41.4 0.4 forward_y.1
  41.8 14.4 %all_to_all.16.sums = f32[8,8,256]{2,1,0:T(8,128)S(1)} all-to-all(f32[8,8,256]{2,1,0:T(8,128)S(1)} %get-tuple-element.16), channel_id=1, replica_groups=mesh['y'=8,'x'=8,'h'=16] {'y'}, dimensions={0} | all-to-all | bytes 131072 | tf_op jit(solution)/shard_map/exchange_sums/all_to_all | solution.py:240
  56.2 0.0 copy-done.2
  56.2 0.4 inverse_y.1
  56.6 19.2 %all_to_all.17 = f32[128,2,128]{2,1,0:T(2,128)S(1)} all-to-all(f32[128,2,128]{2,1,0:T(2,128)S(1)} %bitcast.7), channel_id=1, replica_groups=mesh['y'=8,'x'=8,'h'=16] {'x','h'}, dimensions={0} | all-to-all | bytes 262144 | tf_op jit(solution)/shard_map/exchange_back/all_to_all | solution.py:250
  75.8 0.9 %inverse_x.1 = f32[64,512]{1,0:T(8,128)} custom-call(f32[256,128]{1,0:T(8,128)S(1)} %bitcast.8, bf16[4,256,256]{2,1,0:T(8,128)(2,1)S(1)} %copy-done.2), custom_call_target="tpu_custom_call" | custom-call | tf_op jit(solution)/shard_map/inverse_x/pallas_call | solution.py:252
Async XLA Ops:
  0.0 0.7 copy-start.5
  0.0 0.7 copy-start.6
  0.7 1.0 %copy-start = (bf16[4,256,256]{2,1,0:T(8,128)(2,1)S(1)}, bf16[4,256,256]{2,1,0:T(8,128)(2,1)}, u32[]{:S(2)}) copy-start(bf16[4,256,256]{2,1,0:T(8,128)(2,1)} %constant.8.clone.table) | copy-start | bytes 1572868
  1.7 0.9 %copy-start.3 = (f32[2,32,512]{2,1,0:T(8,128)S(1)}, f32[2,32,512]{2,1,0:T(8,128)}, u32[]{:S(2)}) copy-start(f32[2,32,512]{2,1,0:T(8,128)} %param.6) | copy-start | bytes 393220
  2.6 0.7 copy-start.4
  3.3 38.1 %copy-start.1 = (bf16[4,256,256]{2,1,0:T(8,128)(2,1)S(1)}, bf16[4,256,256]{2,1,0:T(8,128)(2,1)}, u32[]{:S(2)}) copy-start(bf16[4,256,256]{2,1,0:T(8,128)(2,1)} %constant.8.clone.table) | copy-start | bytes 1572868
  41.4 14.8 %copy-start.2 = (bf16[4,256,256]{2,1,0:T(8,128)(2,1)S(1)}, bf16[4,256,256]{2,1,0:T(8,128)(2,1)}, u32[]{:S(2)}) copy-start(bf16[4,256,256]{2,1,0:T(8,128)(2,1)} %constant.9.clone.table) | copy-start | bytes 1572868

commit v4 on v2

--- a/solution.py
+++ b/solution.py
@@ -185,7 +185,6 @@
             out_shape=shape(M, 128),
             in_specs=[VMEM, VMEM],
             out_specs=VMEM,
-            compiler_params=SMALL,
         )(source.reshape(64, N), forward)
     with jax.named_scope("exchange_out"):
         pencils = lax.all_to_all(half.reshape(BX * HA, 2, 128), ("x", "h"), 0, 0, tiled=True)

time: 75.6 us -> 74.8 us (0.989)
  local copies, waits for them, and re-layouts: 1.96 us -> 0.02 us
  Pallas kernels: 4.03 us -> 5.16 us
    unnamed x14 -> x10, local copies, waits for them, and re-layouts: 1.96 us -> 0.02 us
    pallas_call x1, Pallas kernels: 0.95 us -> 2.12 us  [on_device(): pl.pallas_call(forward_x, out_shape=shape(M, 128), in_specs=[VMEM, VMEM],...]
where the time goes in v4:
time: 74.8 us; the launch traced here: 74.5 us
  blocking collectives  33.9 us (45%)
  starting transfers between devices  24.6 us (33%)
  waiting for transfers between devices  10.8 us (14%)
  Pallas kernels  5.16 us (7%)
    all_to_all x1, starting transfers between devices, on_device(): lax.all_to_all(half.reshape(BX * HA, 2, 128), ('x', 'h'), 0, 0, tiled=True)  24.6 us
    all_to_all x1, blocking collectives, on_device(): lax.all_to_all(back.reshape(BX * HA, 2, 128), ('x', 'h'), 0, 0, tiled=True)  19.6 us
    all_to_all x1, blocking collectives, on_device(): sums = lax.all_to_all(sums, 'y', 0, 0, tiled=True)  14.3 us
    all_to_all x1, waiting for transfers between devices, on_device(): lax.all_to_all(half.reshape(BX * HA, 2, 128), ('x', 'h'), 0, 0, tiled=True)  10.8 us
    pallas_call x1, Pallas kernels, on_device(): pl.pallas_call(forward_x, out_shape=shape(M, 128), in_specs=[VMEM, VMEM],...  2.12 us
  transfers between devices with their start and end apart: 1, of which 1 were waited for; matrix products, arithmetic and copies ran while one was open for 0% of the time, Pallas kernels for 2%

profile of v4, /device:TPU:1, one launch (start us, length us, event | category | flops | bytes accessed | tf_op | source)
XLA Modules:
  0.0 74.5 jit_solution(3229621976965064713)
XLA Ops:
  0.0 0.0 copy-start
  0.0 2.1 %forward_x.1 = f32[256,128]{1,0:T(8,128)} custom-call(f32[64,512]{1,0:T(8,128)} %bitcast.10, bf16[4,256,256]{2,1,0:T(8,128)(2,1)} %constant.8.clone.table), custom_call_target="tpu_custom_call" | custom-call | tf_op jit(solution)/shard_map/forward_x/pallas_call | solution.py:183
  2.1 0.0 copy-start.2
  2.1 0.0 copy-start.3
  2.1 0.0 copy-start.4
  2.1 24.6 %all-to-all-start = ((f32[128,2,128]{2,1,0:T(2,128)}), f32[128,2,128]{2,1,0:T(2,128)S(1)}, u32[]{:S(2)}, u32[]{:S(2)}) async-start(f32[128,2,128]{2,1,0:T(2,128)} %bitcast.9), calls=%async_computation | async-start | bytes 262144 | tf_op jit(solution)/shard_map/exchange_out/all_to_all | solution.py:190
  26.7 0.0 copy-done.2
  26.7 0.0 copy-done.3
  26.7 0.0 copy-done.4
  26.7 1.4 %coefficients.1 = (f32[16,8,256]{2,1,0:T(8,128)S(1)}, f32[16,8,256]{2,1,0:T(8,128)S(1)}, f32[8,256]{1,0:T(8,128)S(1)}) custom-call(f32[129]{0:T(256)S(1)} %copy-done.4, f32[512]{0:T(512)S(1)} %copy-done.3, f32[8,256]{1,0:T(8,128)S(1)} %copy-done.2), custom_call_target="tpu_custom_call" | custom-call | tf_op jit(solution)/shard_map/coefficients/pallas_call | solution.py:174
  28.1 10.8 %all-to-all-done = f32[128,2,128]{2,1,0:T(2,128)S(1)} async-done(((f32[128,2,128]{2,1,0:T(2,128)}), f32[128,2,128]{2,1,0:T(2,128)S(1)}, u32[]{:S(2)}, u32[]{:S(2)}) %all-to-all-start) | async-done | bytes 131104 | tf_op jit(solution)/shard_map/exchange_out/all_to_all | solution.py:190
  38.9 0.0 copy-done
  38.9 0.0 copy-start.1
  38.9 0.4 forward_y.1
  39.3 14.3 %all_to_all.15.sums = f32[8,8,256]{2,1,0:T(8,128)S(1)} all-to-all(f32[8,8,256]{2,1,0:T(8,128)S(1)} %get-tuple-element.14), channel_id=1, replica_groups=mesh['y'=8,'x'=8,'h'=16] {'y'}, dimensions={0} | all-to-all | bytes 131072 | tf_op jit(solution)/shard_map/exchange_sums/all_to_all | solution.py:200
  53.6 0.0 copy-done.1
  53.6 0.4 inverse_y.1
  54.0 19.6 %all_to_all.16 = f32[128,2,128]{2,1,0:T(2,128)S(1)} all-to-all(f32[128,2,128]{2,1,0:T(2,128)S(1)} %bitcast.7), channel_id=1, replica_groups=mesh['y'=8,'x'=8,'h'=16] {'x','h'}, dimensions={0} | all-to-all | bytes 262144 | tf_op jit(solution)/shard_map/exchange_back/all_to_all | solution.py:210
  73.6 0.9 %inverse_x.1 = f32[64,512]{1,0:T(8,128)} custom-call(f32[256,128]{1,0:T(8,128)S(1)} %bitcast.8, bf16[4,256,256]{2,1,0:T(8,128)(2,1)S(1)} %copy-done.1), custom_call_target="tpu_custom_call" | custom-call | tf_op jit(solution)/shard_map/inverse_x/pallas_call | solution.py:212
Async XLA Ops:
  0.0 38.9 %copy-start = (bf16[4,256,256]{2,1,0:T(8,128)(2,1)S(1)}, bf16[4,256,256]{2,1,0:T(8,128)(2,1)}, u32[]{:S(2)}) copy-start(bf16[4,256,256]{2,1,0:T(8,128)(2,1)} %constant.8.clone.table) | copy-start | bytes 1572868
  2.1 24.6 %copy-start.2 = (f32[8,256]{1,0:T(8,128)S(1)}, f32[8,256]{1,0:T(8,128)}, u32[]{:S(2)}) copy-start(f32[8,256]{1,0:T(8,128)} %constant.11.clone.eigen_y) | copy-start | bytes 24580
  2.1 24.6 %copy-start.3 = (f32[512]{0:T(512)S(1)}, f32[512]{0:T(512)}, u32[]{:S(2)}) copy-start(f32[512]{0:T(512)} %constant.10.clone.eigen) | copy-start | bytes 6148
  2.1 24.6 %copy-start.4 = (f32[129]{0:T(256)S(1)}, f32[129]{0:T(256)}, u32[]{:S(2)}) copy-start(f32[129]{0:T(256)} %faces.1) | copy-start | bytes 1552
  2.1 36.8 %all-to-all-start = ((f32[128,2,128]{2,1,0:T(2,128)}), f32[128,2,128]{2,1,0:T(2,128)S(1)}, u32[]{:S(2)}, u32[]{:S(2)}) async-start(f32[128,2,128]{2,1,0:T(2,128)} %bitcast.9), calls=%async_computation | async-start | bytes 262144 | tf_op jit(solution)/shard_map/exchange_out/all_to_all | solution.py:190
  38.9 14.7 %copy-start.1 = (bf16[4,256,256]{2,1,0:T(8,128)(2,1)S(1)}, bf16[4,256,256]{2,1,0:T(8,128)(2,1)}, u32[]{:S(2)}) copy-start(bf16[4,256,256]{2,1,0:T(8,128)(2,1)} %constant.9.clone.table) | copy-start | bytes 1572868

commit v5 on v4

v5 whole, which is shorter than its diff:
```python
import math

import jax
import jax.numpy as jnp
import ml_dtypes
import numpy as np
from jax import lax
from jax.experimental import pallas as pl
from jax.experimental.pallas import tpu as pltpu
from jax.sharding import Mesh, PartitionSpec as P

N = 512
M = N // 2
NZ = 128
NY = 8
NX = 8
BX = 4
BLOCKS = NZ // (2 * BX)
BLOCK = NZ // BLOCKS
HA = 16
WAVES = N // (BX * HA)
F32 = jnp.float32
BF16 = jnp.bfloat16


def tables():
    j = np.arange(M)
    def cas(phase):
        t = 2.0 * np.pi * (phase % N) / N
        return (np.cos(t) + np.sin(t)) / math.sqrt(N)
    even = cas(2 * j[:, None] * j[None, :])
    odd = cas((2 * j[:, None] + 1) * j[None, :])
    def split(a):
        hi = a.astype(ml_dtypes.bfloat16)
        return [hi, (a - hi.astype(np.float64)).astype(ml_dtypes.bfloat16)]
    forward = np.stack(split(even) + split(odd.T))
    inverse = np.stack(split(even) + split(odd))
    eigen = 2.0 - 2.0 * np.cos(2.0 * np.pi * np.arange(N) / N)
    parity = (np.arange(16) // 4) % 2
    eigen_y = eigen[2 * j[None, :] + parity[:, None]]
    return forward, inverse, eigen.astype(np.float32), eigen_y.astype(np.float32)


def product(value, high, low):
    top = value.astype(BF16)
    rest = (value - top.astype(F32)).astype(BF16)
    rows = value.shape[0]
    both = jnp.dot(jnp.concatenate([top, rest], 0), high, preferred_element_type=F32)
    return both[:rows] + both[rows:] + jnp.dot(top, low, preferred_element_type=F32)


def swap_blocks(value):
    row = lax.broadcasted_iota(jnp.int32, value.shape, 1) // 4
    lane = lax.broadcasted_iota(jnp.int32, value.shape, 2) // 32
    which = (row - lane) & 3
    out = value
    for s in range(1, 4):
        moved = pltpu.roll(pltpu.roll(value, 4 * s, 1), 128 - 32 * s, 2)
        out = jnp.where(which == s, moved, out)
    return out


def lower_half(shape):
    return lax.broadcasted_iota(jnp.int32, shape, 1) < 4


def place(index):
    return index + lax.axis_index("x1") * (BX - 1 - 2 * index)


def own_block():
    return 2 * lax.axis_index("y") + lax.axis_index("x1")


def block_at(position):
    return 2 * (position % NY) + position // NY


def forward_x(source, table, out):
    value = source[...]
    left, right = value[:, :M], value[:, M:]
    even = product(left + right, table[0], table[1])
    odd = product(left - right, table[2], table[3])
    half = jnp.concatenate([even, odd], 0).T
    for share in range(BX):
        out[pl.ds(place(share) * 64, 64)] = half[share * 64 : (share + 1) * 64]


def inverse_x(spectral, table, out):
    shares = [spectral[pl.ds(place(share) * 64, 64)] for share in range(BX)]
    value = jnp.concatenate(shares, 0).T
    even = product(value[:64], table[0], table[1])
    odd = product(value[64:], table[2], table[3])
    out[:, :M] = even + odd
    out[:, M:] = even - odd


def coefficients(faces, eigen, eigen_y, up_out, down_out, weight_out, ups, downs):
    first = WAVES * (place(lax.axis_index("x2")) * HA + lax.axis_index("h"))
    row = lax.broadcasted_iota(jnp.int32, (16, M), 0)
    wave = 2 * (row & 3) + (row >> 3)
    shift = eigen_y[...]
    for e in range(WAVES):
        shift = shift + jnp.where(wave == e, eigen[first + e], 0.0)

    def inv(index):
        part = 1.0 / jnp.full((8, 128), faces[index], F32)
        part = jnp.concatenate([part, part], 1)
        return jnp.concatenate([part, part], 0)

    def steps(i, carry):
        p, u, q, w = carry
        for k in range(8):
            z = i * 8 + k
            p = p + inv(z) * u
            u = u + shift * p
            ups[z] = p
            q = q + inv(NZ - z) * w
            w = w + shift * q
            downs[NZ - 1 - z] = q
        return p, u, q, w

    zero = jnp.zeros((16, M), F32)
    one = jnp.ones((16, M), F32)
    p, u, q, w = lax.fori_loop(0, NZ // 8, steps, (zero, one, zero, one))
    weight_out[...] = 1.0 / (p + inv(NZ) * u)
    base = own_block() * BLOCK
    up_out[...] = ups[pl.ds(base, BLOCK)]
    down_out[...] = downs[pl.ds(base, BLOCK)]


def forward_y(received, table, ups, downs, weight, local, sums):
    value = received[...].reshape(BX, 2, 2, 16, 128)
    low, high = value[:, 0], value[:, 1]

    def lines(part):
        part = swap_blocks(part.reshape(BX * 2, 16, 128)).reshape(BX, 2, 16, 128)
        return jnp.concatenate([part[:, 0].reshape(64, 128), part[:, 1].reshape(64, 128)], 1)

    even = product(lines(low + high), table[0], table[1]).reshape(8, 8, M)
    odd = product(lines(low - high), table[2], table[3]).reshape(8, 8, M)
    mask = lower_half((8, 8, M))
    lower = jnp.where(mask, even, pltpu.roll(odd, 4, 1)).reshape(BX, 16, M)
    upper = jnp.where(mask, pltpu.roll(even, 4, 1), odd).reshape(BX, 16, M)
    scale = weight[...]
    rows = [(lower if j % 2 == 0 else upper)[j // 2] * scale for j in range(BLOCK)]
    above = [None] * BLOCK
    total_q = jnp.zeros((16, M), F32)
    for j in reversed(range(BLOCK)):
        above[j] = total_q
        total_q = total_q + downs[j] * rows[j]
    total_p = jnp.zeros((16, M), F32)
    for j in range(BLOCK):
        total_p = total_p + ups[j] * rows[j]
        local[j] = downs[j] * total_p + ups[j] * above[j]
    me = own_block()
    for n in range(BLOCKS):
        sums[n] = jnp.where(block_at(n) > me, total_p, total_q)


def inverse_y(local, ups, downs, sums, table, out):
    me = own_block()
    below = jnp.zeros((16, M), F32)
    above = jnp.zeros((16, M), F32)
    for n in range(BLOCKS):
        below = below + jnp.where(block_at(n) < me, sums[n], 0.0)
        above = above + jnp.where(block_at(n) > me, sums[n], 0.0)
    value = local[...] + downs[...] * below + ups[...] * above
    value = value.reshape(BX, 2, 16, M)
    lower, upper = value[:, 0].reshape(8, 8, M), value[:, 1].reshape(8, 8, M)
    mask = lower_half((8, 8, M))
    even = jnp.where(mask, lower, pltpu.roll(upper, 4, 1)).reshape(64, M)
    odd = jnp.where(mask, pltpu.roll(lower, 4, 1), upper).reshape(64, M)
    even = product(even, table[0], table[1])
    odd = product(odd, table[2], table[3])
    for half, part in enumerate((even + odd, even - odd)):
        for side in range(2):
            piece = part[:, side * 128 : (side + 1) * 128].reshape(BX, 16, 128)
            out[:, half, side] = swap_blocks(piece)


def shape(*dims):
    return jax.ShapeDtypeStruct(dims, F32)


VMEM = pl.BlockSpec(memory_space=pltpu.VMEM)
SMALL = pltpu.CompilerParams(vmem_limit_bytes=12 * 1024 * 1024)
SMEM = pl.BlockSpec(memory_space=pltpu.SMEM)


def on_device(source, faces):
    forward, inverse, eigen, eigen_y = (jnp.asarray(t) for t in tables())
    with jax.named_scope("coefficients"):
        ups, downs, weight = pl.pallas_call(
            coefficients,
            out_shape=(shape(BLOCK, 16, M), shape(BLOCK, 16, M), shape(16, M)),
            in_specs=[SMEM, SMEM, VMEM],
            out_specs=(VMEM, VMEM, VMEM),
            scratch_shapes=[pltpu.VMEM((NZ, 16, M), F32), pltpu.VMEM((NZ, 16, M), F32)],
            compiler_params=SMALL,
        )(faces, eigen, eigen_y)
    with jax.named_scope("forward_x"):
        half = pl.pallas_call(
            forward_x,
            out_shape=shape(M, 128),
            in_specs=[VMEM, VMEM],
            out_specs=VMEM,
        )(source.reshape(64, N), forward)
    with jax.named_scope("exchange_out"):
        pencils = lax.all_to_all(half.reshape(BX * HA, 4, 128), ("x2", "h"), 0, 0, tiled=True)
    with jax.named_scope("forward_y"):
        local, sums = pl.pallas_call(
            forward_y,
            out_shape=(shape(BLOCK, 16, M), shape(BLOCKS, 16, M)),
            in_specs=[VMEM] * 5,
            out_specs=(VMEM, VMEM),
            compiler_params=SMALL,
        )(pencils.reshape(M, 128), forward, ups, downs, weight)
    with jax.named_scope("exchange_sums"):
        groups = [[y * NX + x for x in (k, NX - 1 - k) for y in range(NY)] for k in range(BX)]
        sums = lax.all_to_all(
            sums, ("y", "x1", "x2"), 0, 0, tiled=True, axis_index_groups=groups
        )
    with jax.named_scope("inverse_y"):
        back = pl.pallas_call(
            inverse_y,
            out_shape=shape(BX, 2, 2, 16, 128),
            in_specs=[VMEM] * 5,
            out_specs=VMEM,
            compiler_params=SMALL,
        )(local, ups, downs, sums, inverse)
    with jax.named_scope("exchange_back"):
        grid = lax.all_to_all(back.reshape(BX * HA, 4, 128), ("x2", "h"), 0, 0, tiled=True)
    with jax.named_scope("inverse_x"):
        out = pl.pallas_call(
            inverse_x,
            out_shape=shape(64, N),
            in_specs=[VMEM, VMEM],
            out_specs=VMEM,
            compiler_params=SMALL,
        )(grid.reshape(M, 128), inverse)
    return out.reshape(2, 32, N)


def solution(mesh):
    fine = Mesh(mesh.devices.reshape(NY, 2, BX, HA), ("y", "x1", "x2", "h"))
    spec = P(("y", "x1", "x2"), "h", None)
    return jax.shard_map(
        on_device, mesh=fine, in_specs=(spec, P()), out_specs=spec, check_vma=False
    )
```

time: 74.8 us -> 72.2 us (0.965)
  starting transfers between devices: 24.6 us -> 21.7 us
  blocking collectives: 33.9 us -> 36.4 us
  waiting for transfers between devices: 10.8 us -> 8.42 us
    all_to_all x1, starting transfers between devices: 24.6 us -> 21.7 us  [on_device(): lax.all_to_all(half.reshape(BX * HA, 4, 128), ('x2', 'h'), 0, 0, tiled=True)]
    all_to_all x2, blocking collectives: 33.9 us -> 36.4 us  [the longest x1 18.7 us: on_device(): lax.all_to_all(back.reshape(BX * HA, 4, 128), ('x2', 'h'), 0, 0, tiled=True)]
    all_to_all x1, waiting for transfers between devices: 10.8 us -> 8.42 us  [on_device(): lax.all_to_all(half.reshape(BX * HA, 4, 128), ('x2', 'h'), 0, 0, tiled=True)]
where the time goes in v5:
time: 72.2 us; the launch traced here: 71.9 us
  blocking collectives  36.4 us (50%)
  starting transfers between devices  21.7 us (30%)
  waiting for transfers between devices  8.42 us (12%)
  Pallas kernels  5.37 us (7%)
    all_to_all x1, starting transfers between devices, on_device(): lax.all_to_all(half.reshape(BX * HA, 4, 128), ('x2', 'h'), 0, 0, tiled=True)  21.7 us
    all_to_all x1, blocking collectives, on_device(): lax.all_to_all(back.reshape(BX * HA, 4, 128), ('x2', 'h'), 0, 0, tiled=True)  18.7 us
    all_to_all x1, blocking collectives, on_device(): lax.all_to_all(sums, ('y', 'x1', 'x2'), 0, 0, tiled=True, axis_index_grou...  17.7 us
    all_to_all x1, waiting for transfers between devices, on_device(): lax.all_to_all(half.reshape(BX * HA, 4, 128), ('x2', 'h'), 0, 0, tiled=True)  8.42 us
    pallas_call x1, Pallas kernels, on_device(): pl.pallas_call(forward_x, out_shape=shape(M, 128), in_specs=[VMEM, VMEM],...  2.12 us
    pallas_call x1, Pallas kernels, on_device(): pl.pallas_call(coefficients, out_shape=(shape(BLOCK, 16, M), shape(BLOCK,...  1.53 us
  transfers between devices with their start and end apart: 1, of which 1 were waited for; matrix products, arithmetic and copies ran while one was open for 0% of the time, Pallas kernels for 2%

profile of v5, /device:TPU:1, one launch (start us, length us, event | category | flops | bytes accessed | tf_op | source)
XLA Modules:
  0.0 71.9 jit_solution(4335027799425470308)
XLA Ops:
  0.0 0.0 copy-start
  0.0 2.1 %forward_x.1 = f32[256,128]{1,0:T(8,128)} custom-call(f32[64,512]{1,0:T(8,128)} %bitcast.10, bf16[4,256,256]{2,1,0:T(8,128)(2,1)} %constant.8.clone.table), custom_call_target="tpu_custom_call" | custom-call | tf_op jit(solution)/shard_map/forward_x/pallas_call | solution.py:203
  2.1 0.0 copy-start.2
  2.1 0.0 copy-start.3
  2.1 0.0 copy-start.4
  2.1 21.7 %all-to-all-start = ((f32[64,4,128]{2,1,0:T(4,128)}), f32[64,4,128]{2,1,0:T(4,128)S(1)}, u32[]{:S(2)}, u32[]{:S(2)}) async-start(f32[64,4,128]{2,1,0:T(4,128)} %bitcast.9), calls=%async_computation | async-start | bytes 262144 | tf_op jit(solution)/shard_map/exchange_out/all_to_all | solution.py:210
  23.8 0.0 copy-done.2
  23.8 0.0 copy-done.3
  23.8 0.0 copy-done.4
  23.8 1.5 %coefficients.1 = (f32[8,16,256]{2,1,0:T(8,128)S(1)}, f32[8,16,256]{2,1,0:T(8,128)S(1)}, f32[16,256]{1,0:T(8,128)S(1)}) custom-call(f32[129]{0:T(256)S(1)} %copy-done.4, f32[512]{0:T(512)S(1)} %copy-done.3, f32[16,256]{1,0:T(8,128)S(1)} %copy-done.2), custom_call_target="tpu_custom_call" | custom-call | tf_op jit(solution)/shard_map/coefficients/pallas_call | solution.py:194
  25.4 8.4 %all-to-all-done = f32[64,4,128]{2,1,0:T(4,128)S(1)} async-done(((f32[64,4,128]{2,1,0:T(4,128)}), f32[64,4,128]{2,1,0:T(4,128)S(1)}, u32[]{:S(2)}, u32[]{:S(2)}) %all-to-all-start) | async-done | bytes 131104 | tf_op jit(solution)/shard_map/exchange_out/all_to_all | solution.py:210
  33.8 0.0 copy-done
  33.8 0.0 copy-start.1
  33.8 0.4 forward_y.1
  34.2 17.7 %all_to_all.15.sums = f32[16,16,256]{2,1,0:T(8,128)S(1)} all-to-all(f32[16,16,256]{2,1,0:T(8,128)S(1)} %get-tuple-element.14), channel_id=1, replica_groups={{0,128,256,384,512,640,768,896,112,240,368,496,624,752,880,1008},{16,14..., dimensions={0} | all-to-all | bytes 524288 | tf_op jit(solution)/shard_map/exchange_sums/all_to_all | solution.py:221
  51.9 0.0 copy-done.1
  51.9 0.4 inverse_y.1
  52.3 18.7 %all_to_all.16 = f32[64,4,128]{2,1,0:T(4,128)S(1)} all-to-all(f32[64,4,128]{2,1,0:T(4,128)S(1)} %bitcast.7), channel_id=1, replica_groups=mesh['y'=8,'x1'=2,'x2'=4,'h'=16] {'x2','h'}, dimensions={0} | all-to-all | bytes 262144 | tf_op jit(solution)/shard_map/exchange_back/all_to_all | solution.py:233
  71.0 0.9 %inverse_x.1 = f32[64,512]{1,0:T(8,128)} custom-call(f32[256,128]{1,0:T(8,128)S(1)} %bitcast.8, bf16[4,256,256]{2,1,0:T(8,128)(2,1)S(1)} %copy-done.1), custom_call_target="tpu_custom_call" | custom-call | tf_op jit(solution)/shard_map/inverse_x/pallas_call | solution.py:235
Async XLA Ops:
  0.0 33.8 %copy-start = (bf16[4,256,256]{2,1,0:T(8,128)(2,1)S(1)}, bf16[4,256,256]{2,1,0:T(8,128)(2,1)}, u32[]{:S(2)}) copy-start(bf16[4,256,256]{2,1,0:T(8,128)(2,1)} %constant.8.clone.table) | copy-start | bytes 1572868
  2.1 21.7 %copy-start.2 = (f32[16,256]{1,0:T(8,128)S(1)}, f32[16,256]{1,0:T(8,128)}, u32[]{:S(2)}) copy-start(f32[16,256]{1,0:T(8,128)} %constant.11.clone.eigen_y) | copy-start | bytes 49156
  2.1 21.7 %copy-start.3 = (f32[512]{0:T(512)S(1)}, f32[512]{0:T(512)}, u32[]{:S(2)}) copy-start(f32[512]{0:T(512)} %constant.10.clone.eigen) | copy-start | bytes 6148
  2.1 21.7 %copy-start.4 = (f32[129]{0:T(256)S(1)}, f32[129]{0:T(256)}, u32[]{:S(2)}) copy-start(f32[129]{0:T(256)} %faces.1) | copy-start | bytes 1552
  2.1 31.6 %all-to-all-start = ((f32[64,4,128]{2,1,0:T(4,128)}), f32[64,4,128]{2,1,0:T(4,128)S(1)}, u32[]{:S(2)}, u32[]{:S(2)}) async-start(f32[64,4,128]{2,1,0:T(4,128)} %bitcast.9), calls=%async_computation | async-start | bytes 262144 | tf_op jit(solution)/shard_map/exchange_out/all_to_all | solution.py:210
  33.8 18.1 %copy-start.1 = (bf16[4,256,256]{2,1,0:T(8,128)(2,1)S(1)}, bf16[4,256,256]{2,1,0:T(8,128)(2,1)}, u32[]{:S(2)}) copy-start(bf16[4,256,256]{2,1,0:T(8,128)(2,1)} %constant.9.clone.table) | copy-start | bytes 1572868

commit v6 on v5

--- a/solution.py
+++ b/solution.py
@@ -76,8 +76,23 @@
     return 2 * (position % NY) + position // NY
 
 
-def forward_x(source, table, out):
-    value = source[...]
+def forward_x(
+    source, matrices, faces, eigen, eigen_y, out, up_out, down_out, weight_out,
+    value, table, face, wave_x, wave_y, ps, us, qs, ws, sems,
+):
+    copies = [
+        pltpu.make_async_copy(src, dst, sems.at[n])
+        for n, (src, dst) in enumerate(
+            ((faces, face), (eigen, wave_x), (eigen_y, wave_y), (source, value), (matrices, table))
+        )
+    ]
+    for copy in copies:
+        copy.start()
+    for copy in copies[:3]:
+        copy.wait()
+    coefficients(face, wave_x, wave_y, up_out, down_out, weight_out, ps, us, qs, ws)
+    for copy in copies[3:]:
+        copy.wait()
     left, right = value[:, :M], value[:, M:]
     even = product(left + right, table[0], table[1])
     odd = product(left - right, table[2], table[3])
@@ -95,7 +110,7 @@
     out[:, M:] = even - odd
 
 
-def coefficients(faces, eigen, eigen_y, up_out, down_out, weight_out, ups, downs):
+def coefficients(faces, eigen, eigen_y, up_out, down_out, weight_out, ps, us, qs, ws):
     first = WAVES * (place(lax.axis_index("x2")) * HA + lax.axis_index("h"))
     row = lax.broadcasted_iota(jnp.int32, (16, M), 0)
     wave = 2 * (row & 3) + (row >> 3)
@@ -108,25 +123,41 @@
         part = jnp.concatenate([part, part], 1)
         return jnp.concatenate([part, part], 0)
 
-    def steps(i, carry):
-        p, u, q, w = carry
-        for k in range(8):
-            z = i * 8 + k
-            p = p + inv(z) * u
-            u = u + shift * p
-            ups[z] = p
-            q = q + inv(NZ - z) * w
-            w = w + shift * q
-            downs[NZ - 1 - z] = q
-        return p, u, q, w
-
-    zero = jnp.zeros((16, M), F32)
-    one = jnp.ones((16, M), F32)
-    p, u, q, w = lax.fori_loop(0, NZ // 8, steps, (zero, one, zero, one))
-    weight_out[...] = 1.0 / (p + inv(NZ) * u)
-    base = own_block() * BLOCK
-    up_out[...] = ups[pl.ds(base, BLOCK)]
-    down_out[...] = downs[pl.ds(base, BLOCK)]
+    blocks = [None] * BLOCKS
+    for b in range(0, BLOCKS, 2):
+        for c in (b, b + 1):
+            g = inv(c * BLOCK)
+            blocks[c] = (jnp.ones((16, M), F32), g, shift, 1.0 + shift * g)
+        for j in range(1, BLOCK):
+            for c in (b, b + 1):
+                pa, pb, ua, ub = blocks[c]
+                g = inv(c * BLOCK + j)
+                pa, pb = pa + g * ua, pb + g * ub
+                blocks[c] = (pa, pb, ua + shift * pa, ub + shift * pb)
+    last = inv(NZ)
+    p, u = jnp.zeros((16, M), F32), jnp.ones((16, M), F32)
+    q, w = last, jnp.ones((16, M), F32)
+    for b in range(BLOCKS):
+        ps[b], us[b] = p, u
+        pa, pb, ua, ub = blocks[b]
+        p, u = pa * p + pb * u, ua * p + ub * u
+        c = BLOCKS - 1 - b
+        qs[c], ws[c] = q, w
+        pa, pb, ua, ub = blocks[c]
+        q, w = ub * q + pb * w, ua * q + pa * w
+    weight_out[...] = 1.0 / (p + last * u)
+
+    me = own_block()
+    inner = [inv(me * BLOCK + j) for j in range(BLOCK)]
+    p, u, q, w = ps[me], us[me], qs[me], ws[me]
+    for j in range(BLOCK):
+        p = p + inner[j] * u
+        up_out[j] = p
+        u = u + shift * p
+        k = BLOCK - 1 - j
+        down_out[k] = q
+        w = w + shift * q
+        q = q + inner[k] * w
 
 
 def forward_y(received, table, ups, downs, weight, local, sums):
@@ -185,27 +216,29 @@
 
 VMEM = pl.BlockSpec(memory_space=pltpu.VMEM)
 SMALL = pltpu.CompilerParams(vmem_limit_bytes=12 * 1024 * 1024)
-SMEM = pl.BlockSpec(memory_space=pltpu.SMEM)
+HBM = pl.BlockSpec(memory_space=pltpu.HBM)
 
 
 def on_device(source, faces):
     forward, inverse, eigen, eigen_y = (jnp.asarray(t) for t in tables())
-    with jax.named_scope("coefficients"):
-        ups, downs, weight = pl.pallas_call(
-            coefficients,
-            out_shape=(shape(BLOCK, 16, M), shape(BLOCK, 16, M), shape(16, M)),
-            in_specs=[SMEM, SMEM, VMEM],
-            out_specs=(VMEM, VMEM, VMEM),
-            scratch_shapes=[pltpu.VMEM((NZ, 16, M), F32), pltpu.VMEM((NZ, 16, M), F32)],
-            compiler_params=SMALL,
-        )(faces, eigen, eigen_y)
     with jax.named_scope("forward_x"):
-        half = pl.pallas_call(
+        operands = (source.reshape(64, N), forward, faces, eigen, eigen_y)
+        half, ups, downs, weight = pl.pallas_call(
             forward_x,
-            out_shape=shape(M, 128),
-            in_specs=[VMEM, VMEM],
-            out_specs=VMEM,
-        )(source.reshape(64, N), forward)
+            out_shape=(shape(M, 128), shape(BLOCK, 16, M), shape(BLOCK, 16, M), shape(16, M)),
+            in_specs=[HBM] * 5,
+            out_specs=(VMEM,) * 4,
+            scratch_shapes=[
+                pltpu.VMEM((64, N), F32),
+                pltpu.VMEM((4, M, M), BF16),
+                pltpu.SMEM((NZ + 1,), F32),
+                pltpu.SMEM((N,), F32),
+                pltpu.VMEM((16, M), F32),
+                *[pltpu.VMEM((BLOCKS, 16, M), F32)] * 4,
+                pltpu.SemaphoreType.DMA((5,)),
+            ],
+            compiler_params=SMALL,
+        )(*[pltpu.with_memory_space_constraint(x, pltpu.HBM) for x in operands])
     with jax.named_scope("exchange_out"):
         pencils = lax.all_to_all(half.reshape(BX * HA, 4, 128), ("x2", "h"), 0, 0, tiled=True)
     with jax.named_scope("forward_y"):

time: 72.2 us -> 71.6 us (level)
  blocking collectives: 36.4 us -> 67.7 us
  starting transfers between devices: 21.7 us -> 0 us
  waiting for transfers between devices: 8.42 us -> 0 us
  Pallas kernels: 5.37 us -> 3.63 us
    all_to_all x0 -> x1, blocking collectives: none -> 31.3 us  [on_device(): lax.all_to_all(half.reshape(BX * HA, 4, 128), ('x2', 'h'), 0, 0, tiled=True)]
    all_to_all x1 -> x0, starting transfers between devices: 21.7 us -> none  [on_device(): lax.all_to_all(half.reshape(BX * HA, 4, 128), ('x2', 'h'), 0, 0, tiled=True)]
    all_to_all x1 -> x0, waiting for transfers between devices: 8.42 us -> none  [on_device(): lax.all_to_all(half.reshape(BX * HA, 4, 128), ('x2', 'h'), 0, 0, tiled=True)]
    pallas_call x2 -> x1, Pallas kernels: 3.65 us -> 1.9 us  [on_device(): pl.pallas_call(forward_x, out_shape=(shape(M, 128), shape(BLOCK, 16, M),...]
  transfers between devices with their start and end apart: 1 -> 0, of which waited for: 1 -> 0; matrix products, arithmetic and copies ran while one was open for 0% -> 0% of each run, Pallas kernels for 2% -> 0%
where the time goes in v6:
time: 71.6 us; the launch traced here: 71.4 us
  blocking collectives  67.7 us (95%)
  Pallas kernels  3.63 us (5%)
    all_to_all x1, blocking collectives, on_device(): lax.all_to_all(half.reshape(BX * HA, 4, 128), ('x2', 'h'), 0, 0, tiled=True)  31.3 us
    all_to_all x1, blocking collectives, on_device(): lax.all_to_all(back.reshape(BX * HA, 4, 128), ('x2', 'h'), 0, 0, tiled=True)  18.7 us
    all_to_all x1, blocking collectives, on_device(): lax.all_to_all(sums, ('y', 'x1', 'x2'), 0, 0, tiled=True, axis_index_grou...  17.7 us
    pallas_call x1, Pallas kernels, on_device(): pl.pallas_call(forward_x, out_shape=(shape(M, 128), shape(BLOCK, 16, M),...  1.9 us

profile of v6, /device:TPU:1, one launch (start us, length us, event | category | flops | bytes accessed | tf_op | source)
XLA Modules:
  0.0 71.4 jit_solution(12530247510612345319)
XLA Ops:
  0.0 0.0 copy-start
  0.0 1.9 %forward_x.1 = (f32[256,128]{1,0:T(8,128)S(1)}, f32[8,16,256]{2,1,0:T(8,128)S(1)}, f32[8,16,256]{2,1,0:T(8,128)S(1)}, f32[16,256]{1,0:T(8,128)S(1)}) custom-call(f32[64,512]{1,0:T(8,128)} %bitcast.10, bf16[4,256,256]{2,1,0:T(8,128)(2,1)} %constant.8.clone.matrices.table, f32[129]{0:T(256)} %faces.1, f32[512]{0:T(512)} %constant.10.clone.eigen, ...), custom_call_target="tpu_custom_call" | custom-call | tf_op jit(solution)/shard_map/forward_x/pallas_call | solution.py:226
  1.9 31.3 %all_to_all.15 = f32[64,4,128]{2,1,0:T(4,128)S(1)} all-to-all(f32[64,4,128]{2,1,0:T(4,128)S(1)} %bitcast.9), channel_id=1, replica_groups=mesh['y'=8,'x1'=2,'x2'=4,'h'=16] {'x2','h'}, dimensions={0} | all-to-all | bytes 262144 | tf_op jit(solution)/shard_map/exchange_out/all_to_all | solution.py:243
  33.2 0.0 copy-done
  33.2 0.0 copy-start.1
  33.2 0.4 forward_y.1
  33.6 17.7 %all_to_all.16.sums = f32[16,16,256]{2,1,0:T(8,128)S(1)} all-to-all(f32[16,16,256]{2,1,0:T(8,128)S(1)} %get-tuple-element.16), channel_id=1, replica_groups={{0,128,256,384,512,640,768,896,112,240,368,496,624,752,880,1008},{16,14..., dimensions={0} | all-to-all | bytes 524288 | tf_op jit(solution)/shard_map/exchange_sums/all_to_all | solution.py:254
  51.3 0.0 copy-done.1
  51.3 0.4 inverse_y.1
  51.8 18.7 %all_to_all.17 = f32[64,4,128]{2,1,0:T(4,128)S(1)} all-to-all(f32[64,4,128]{2,1,0:T(4,128)S(1)} %bitcast.7), channel_id=1, replica_groups=mesh['y'=8,'x1'=2,'x2'=4,'h'=16] {'x2','h'}, dimensions={0} | all-to-all | bytes 262144 | tf_op jit(solution)/shard_map/exchange_back/all_to_all | solution.py:266
  70.4 0.9 %inverse_x.1 = f32[64,512]{1,0:T(8,128)} custom-call(f32[256,128]{1,0:T(8,128)S(1)} %bitcast.8, bf16[4,256,256]{2,1,0:T(8,128)(2,1)S(1)} %copy-done.1), custom_call_target="tpu_custom_call" | custom-call | tf_op jit(solution)/shard_map/inverse_x/pallas_call | solution.py:268
Async XLA Ops:
  0.0 33.2 %copy-start = (bf16[4,256,256]{2,1,0:T(8,128)(2,1)S(1)}, bf16[4,256,256]{2,1,0:T(8,128)(2,1)}, u32[]{:S(2)}) copy-start(bf16[4,256,256]{2,1,0:T(8,128)(2,1)} %constant.8.clone.matrices.table) | copy-start | bytes 1572868
  33.2 18.1 %copy-start.1 = (bf16[4,256,256]{2,1,0:T(8,128)(2,1)S(1)}, bf16[4,256,256]{2,1,0:T(8,128)(2,1)}, u32[]{:S(2)}) copy-start(bf16[4,256,256]{2,1,0:T(8,128)(2,1)} %constant.9.clone.table) | copy-start | bytes 1572868

commit v7 on v6

--- a/solution.py
+++ b/solution.py
@@ -77,8 +77,8 @@
 
 
 def forward_x(
-    source, matrices, faces, eigen, eigen_y, out, up_out, down_out, weight_out,
-    value, table, face, wave_x, wave_y, ps, us, qs, ws, sems,
+    source, matrices, faces, eigen, eigen_y, out, up_out, down_out, weight_out, table,
+    value, face, wave_x, wave_y, ps, us, qs, ws, sems,
 ):
     copies = [
         pltpu.make_async_copy(src, dst, sems.at[n])
@@ -90,7 +90,7 @@
         copy.start()
     for copy in copies[:3]:
         copy.wait()
-    coefficients(face, wave_x, wave_y, up_out, down_out, weight_out, ps, us, qs, ws)
+    shift, blocks, inv = block_matrices(face, wave_x, wave_y)
     for copy in copies[3:]:
         copy.wait()
     left, right = value[:, :M], value[:, M:]
@@ -99,6 +99,7 @@
     half = jnp.concatenate([even, odd], 0).T
     for share in range(BX):
         out[pl.ds(place(share) * 64, 64)] = half[share * 64 : (share + 1) * 64]
+    coefficients(shift, blocks, inv, up_out, down_out, weight_out, ps, us, qs, ws)
 
 
 def inverse_x(spectral, table, out):
@@ -110,7 +111,7 @@
     out[:, M:] = even - odd
 
 
-def coefficients(faces, eigen, eigen_y, up_out, down_out, weight_out, ps, us, qs, ws):
+def block_matrices(faces, eigen, eigen_y):
     first = WAVES * (place(lax.axis_index("x2")) * HA + lax.axis_index("h"))
     row = lax.broadcasted_iota(jnp.int32, (16, M), 0)
     wave = 2 * (row & 3) + (row >> 3)
@@ -134,6 +135,10 @@
                 g = inv(c * BLOCK + j)
                 pa, pb = pa + g * ua, pb + g * ub
                 blocks[c] = (pa, pb, ua + shift * pa, ub + shift * pb)
+    return shift, blocks, inv
+
+
+def coefficients(shift, blocks, inv, up_out, down_out, weight_out, ps, us, qs, ws):
     last = inv(NZ)
     p, u = jnp.zeros((16, M), F32), jnp.ones((16, M), F32)
     q, w = last, jnp.ones((16, M), F32)
@@ -223,14 +228,19 @@
     forward, inverse, eigen, eigen_y = (jnp.asarray(t) for t in tables())
     with jax.named_scope("forward_x"):
         operands = (source.reshape(64, N), forward, faces, eigen, eigen_y)
-        half, ups, downs, weight = pl.pallas_call(
+        half, ups, downs, weight, table = pl.pallas_call(
             forward_x,
-            out_shape=(shape(M, 128), shape(BLOCK, 16, M), shape(BLOCK, 16, M), shape(16, M)),
+            out_shape=(
+                shape(M, 128),
+                shape(BLOCK, 16, M),
+                shape(BLOCK, 16, M),
+                shape(16, M),
+                jax.ShapeDtypeStruct((4, M, M), BF16),
+            ),
             in_specs=[HBM] * 5,
-            out_specs=(VMEM,) * 4,
+            out_specs=(VMEM,) * 5,
             scratch_shapes=[
                 pltpu.VMEM((64, N), F32),
-                pltpu.VMEM((4, M, M), BF16),
                 pltpu.SMEM((NZ + 1,), F32),
                 pltpu.SMEM((N,), F32),
                 pltpu.VMEM((16, M), F32),
@@ -248,7 +258,7 @@
             in_specs=[VMEM] * 5,
             out_specs=(VMEM, VMEM),
             compiler_params=SMALL,
-        )(pencils.reshape(M, 128), forward, ups, downs, weight)
+        )(pencils.reshape(M, 128), table, ups, downs, weight)
     with jax.named_scope("exchange_sums"):
         groups = [[y * NX + x for x in (k, NX - 1 - k) for y in range(NY)] for k in range(BX)]
         sums = lax.all_to_all(

time: 71.6 us -> 71.4 us (level)
  no operation moved by 1% of the time
where the time goes in v7:
time: 71.4 us; the launch traced here: 71.2 us
  blocking collectives  67.7 us (95%)
  Pallas kernels  3.49 us (5%)
    all_to_all x1, blocking collectives, on_device(): lax.all_to_all(half.reshape(BX * HA, 4, 128), ('x2', 'h'), 0, 0, tiled=True)  31.3 us
    all_to_all x1, blocking collectives, on_device(): lax.all_to_all(back.reshape(BX * HA, 4, 128), ('x2', 'h'), 0, 0, tiled=True)  18.7 us
    all_to_all x1, blocking collectives, on_device(): lax.all_to_all(sums, ('y', 'x1', 'x2'), 0, 0, tiled=True, axis_index_grou...  17.7 us
    pallas_call x1, Pallas kernels, on_device(): pl.pallas_call(forward_x, out_shape=(shape(M, 128), shape(BLOCK, 16, M),...  1.77 us

profile of v7, /device:TPU:1, one launch (start us, length us, event | category | flops | bytes accessed | tf_op | source)
XLA Modules:
  0.0 71.2 jit_solution(6904344637432023348)
XLA Ops:
  0.0 1.8 %forward_x.1 = (f32[256,128]{1,0:T(8,128)S(1)}, f32[8,16,256]{2,1,0:T(8,128)S(1)}, f32[8,16,256]{2,1,0:T(8,128)S(1)}, f32[16,256]{1,0:T(8,128)S(1)}, bf16[4,256,256]{2,1,0:T(8,128)(2,1)S(1)}) custom-call(f32[64,512]{1,0:T(8,128)} %bitcast.10, bf16[4,256,256]{2,1,0:T(8,128)(2,1)} %constant.8.clone.matrices, f32[129]{0:T(256)} %faces.1, ...), custom_call_target="tpu_custom_call" | custom-call | tf_op jit(solution)/shard_map/forward_x/pallas_call | solution.py:231
  1.8 31.3 %all_to_all.15 = f32[64,4,128]{2,1,0:T(4,128)S(1)} all-to-all(f32[64,4,128]{2,1,0:T(4,128)S(1)} %bitcast.9), channel_id=1, replica_groups=mesh['y'=8,'x1'=2,'x2'=4,'h'=16] {'x2','h'}, dimensions={0} | all-to-all | bytes 262144 | tf_op jit(solution)/shard_map/exchange_out/all_to_all | solution.py:253
  33.1 0.0 copy-start
  33.1 0.4 forward_y.1
  33.5 17.7 %all_to_all.16.sums = f32[16,16,256]{2,1,0:T(8,128)S(1)} all-to-all(f32[16,16,256]{2,1,0:T(8,128)S(1)} %get-tuple-element.18), channel_id=1, replica_groups={{0,128,256,384,512,640,768,896,112,240,368,496,624,752,880,1008},{16,14..., dimensions={0} | all-to-all | bytes 524288 | tf_op jit(solution)/shard_map/exchange_sums/all_to_all | solution.py:264
  51.2 0.0 copy-done
  51.2 0.4 inverse_y.1
  51.6 18.7 %all_to_all.17 = f32[64,4,128]{2,1,0:T(4,128)S(1)} all-to-all(f32[64,4,128]{2,1,0:T(4,128)S(1)} %bitcast.7), channel_id=1, replica_groups=mesh['y'=8,'x1'=2,'x2'=4,'h'=16] {'x2','h'}, dimensions={0} | all-to-all | bytes 262144 | tf_op jit(solution)/shard_map/exchange_back/all_to_all | solution.py:276
  70.3 0.9 %inverse_x.1 = f32[64,512]{1,0:T(8,128)} custom-call(f32[256,128]{1,0:T(8,128)S(1)} %bitcast.8, bf16[4,256,256]{2,1,0:T(8,128)(2,1)S(1)} %copy-done), custom_call_target="tpu_custom_call" | custom-call | tf_op jit(solution)/shard_map/inverse_x/pallas_call | solution.py:278
Async XLA Ops:
  33.1 18.1 %copy-start = (bf16[4,256,256]{2,1,0:T(8,128)(2,1)S(1)}, bf16[4,256,256]{2,1,0:T(8,128)(2,1)}, u32[]{:S(2)}) copy-start(bf16[4,256,256]{2,1,0:T(8,128)(2,1)} %constant.9.clone.table) | copy-start | bytes 1572868

commit v8 on v7

--- a/solution.py
+++ b/solution.py
@@ -52,12 +52,11 @@
 def swap_blocks(value):
     row = lax.broadcasted_iota(jnp.int32, value.shape, 1) // 4
     lane = lax.broadcasted_iota(jnp.int32, value.shape, 2) // 32
-    which = (row - lane) & 3
-    out = value
-    for s in range(1, 4):
-        moved = pltpu.roll(pltpu.roll(value, 4 * s, 1), 128 - 32 * s, 2)
-        out = jnp.where(which == s, moved, out)
-    return out
+    far = pltpu.roll(pltpu.roll(value, 8, 1), 64, 2)
+    value = jnp.where(((row ^ lane) & 2) == 0, value, far)
+    near = pltpu.roll(value.reshape(-1, 8, 128), 4, 1).reshape(value.shape)
+    near = jnp.where((lane & 1) == 0, pltpu.roll(near, 96, 2), pltpu.roll(near, 32, 2))
+    return jnp.where(((row ^ lane) & 1) == 0, value, near)
 
 
 def lower_half(shape):

time: 71.4 us -> 71.5 us (level)
  no operation moved by 1% of the time
where the time goes in v8:
time: 71.5 us; the launch traced here: 71.3 us
  blocking collectives  67.7 us (95%)
  Pallas kernels  3.57 us (5%)
    all_to_all x1, blocking collectives, on_device(): lax.all_to_all(half.reshape(BX * HA, 4, 128), ('x2', 'h'), 0, 0, tiled=True)  31.3 us
    all_to_all x1, blocking collectives, on_device(): lax.all_to_all(back.reshape(BX * HA, 4, 128), ('x2', 'h'), 0, 0, tiled=True)  18.6 us
    all_to_all x1, blocking collectives, on_device(): lax.all_to_all(sums, ('y', 'x1', 'x2'), 0, 0, tiled=True, axis_index_grou...  17.7 us
    pallas_call x1, Pallas kernels, on_device(): pl.pallas_call(forward_x, out_shape=(shape(M, 128), shape(BLOCK, 16, M),...  1.77 us

profile of v8, /device:TPU:1, one launch (start us, length us, event | category | flops | bytes accessed | tf_op | source)
XLA Modules:
  0.0 71.3 jit_solution(9047190372854708555)
XLA Ops:
  0.0 1.8 %forward_x.1 = (f32[256,128]{1,0:T(8,128)S(1)}, f32[8,16,256]{2,1,0:T(8,128)S(1)}, f32[8,16,256]{2,1,0:T(8,128)S(1)}, f32[16,256]{1,0:T(8,128)S(1)}, bf16[4,256,256]{2,1,0:T(8,128)(2,1)S(1)}) custom-call(f32[64,512]{1,0:T(8,128)} %bitcast.10, bf16[4,256,256]{2,1,0:T(8,128)(2,1)} %constant.8.clone.matrices, f32[129]{0:T(256)} %faces.1, ...), custom_call_target="tpu_custom_call" | custom-call | tf_op jit(solution)/shard_map/forward_x/pallas_call | solution.py:230
  1.8 31.3 %all_to_all.15 = f32[64,4,128]{2,1,0:T(4,128)S(1)} all-to-all(f32[64,4,128]{2,1,0:T(4,128)S(1)} %bitcast.9), channel_id=1, replica_groups=mesh['y'=8,'x1'=2,'x2'=4,'h'=16] {'x2','h'}, dimensions={0} | all-to-all | bytes 262144 | tf_op jit(solution)/shard_map/exchange_out/all_to_all | solution.py:252
  33.1 0.0 copy-start
  33.1 0.4 forward_y.1
  33.5 17.7 %all_to_all.16.sums = f32[16,16,256]{2,1,0:T(8,128)S(1)} all-to-all(f32[16,16,256]{2,1,0:T(8,128)S(1)} %get-tuple-element.18), channel_id=1, replica_groups={{0,128,256,384,512,640,768,896,112,240,368,496,624,752,880,1008},{16,14..., dimensions={0} | all-to-all | bytes 524288 | tf_op jit(solution)/shard_map/exchange_sums/all_to_all | solution.py:263
  51.2 0.0 copy-done
  51.2 0.5 inverse_y.1
  51.7 18.6 %all_to_all.17 = f32[64,4,128]{2,1,0:T(4,128)S(1)} all-to-all(f32[64,4,128]{2,1,0:T(4,128)S(1)} %bitcast.7), channel_id=1, replica_groups=mesh['y'=8,'x1'=2,'x2'=4,'h'=16] {'x2','h'}, dimensions={0} | all-to-all | bytes 262144 | tf_op jit(solution)/shard_map/exchange_back/all_to_all | solution.py:275
  70.3 0.9 %inverse_x.1 = f32[64,512]{1,0:T(8,128)} custom-call(f32[256,128]{1,0:T(8,128)S(1)} %bitcast.8, bf16[4,256,256]{2,1,0:T(8,128)(2,1)S(1)} %copy-done), custom_call_target="tpu_custom_call" | custom-call | tf_op jit(solution)/shard_map/inverse_x/pallas_call | solution.py:277
Async XLA Ops:
  33.1 18.1 %copy-start = (bf16[4,256,256]{2,1,0:T(8,128)(2,1)S(1)}, bf16[4,256,256]{2,1,0:T(8,128)(2,1)}, u32[]{:S(2)}) copy-start(bf16[4,256,256]{2,1,0:T(8,128)(2,1)} %constant.9.clone.table) | copy-start | bytes 1572868

commit v9 on v7

--- a/solution.py
+++ b/solution.py
@@ -73,7 +73,7 @@
 
 
 def block_at(position):
-    return 2 * (position % NY) + position // NY
+    return 4 * (position // 4) + 2 * (position % 2) + position // 2 % 2
 
 
 def forward_x(
@@ -260,7 +260,10 @@
             compiler_params=SMALL,
         )(pencils.reshape(M, 128), table, ups, downs, weight)
     with jax.named_scope("exchange_sums"):
-        groups = [[y * NX + x for x in (k, NX - 1 - k) for y in range(NY)] for k in range(BX)]
+        groups = [
+            [(y + i) * NX + x for y in range(0, NY, 2) for x in (k, NX - 1 - k) for i in range(2)]
+            for k in range(BX)
+        ]
         sums = lax.all_to_all(
             sums, ("y", "x1", "x2"), 0, 0, tiled=True, axis_index_groups=groups
         )

time: 71.4 us -> 71.4 us (level)
  no operation moved by 1% of the time
where the time goes in v9:
time: 71.4 us; the launch traced here: 71.2 us
  blocking collectives  67.7 us (95%)
  Pallas kernels  3.49 us (5%)
    all_to_all x1, blocking collectives, on_device(): lax.all_to_all(half.reshape(BX * HA, 4, 128), ('x2', 'h'), 0, 0, tiled=True)  31.3 us
    all_to_all x1, blocking collectives, on_device(): lax.all_to_all(back.reshape(BX * HA, 4, 128), ('x2', 'h'), 0, 0, tiled=True)  18.6 us
    all_to_all x1, blocking collectives, on_device(): lax.all_to_all(sums, ('y', 'x1', 'x2'), 0, 0, tiled=True, axis_index_grou...  17.7 us
    pallas_call x1, Pallas kernels, on_device(): pl.pallas_call(forward_x, out_shape=(shape(M, 128), shape(BLOCK, 16, M),...  1.77 us

profile of v9, /device:TPU:1, one launch (start us, length us, event | category | flops | bytes accessed | tf_op | source)
XLA Modules:
  0.0 71.2 jit_solution(3190699156372487191)
XLA Ops:
  0.0 1.8 %forward_x.1 = (f32[256,128]{1,0:T(8,128)S(1)}, f32[8,16,256]{2,1,0:T(8,128)S(1)}, f32[8,16,256]{2,1,0:T(8,128)S(1)}, f32[16,256]{1,0:T(8,128)S(1)}, bf16[4,256,256]{2,1,0:T(8,128)(2,1)S(1)}) custom-call(f32[64,512]{1,0:T(8,128)} %bitcast.10, bf16[4,256,256]{2,1,0:T(8,128)(2,1)} %constant.8.clone.matrices, f32[129]{0:T(256)} %faces.1, ...), custom_call_target="tpu_custom_call" | custom-call | tf_op jit(solution)/shard_map/forward_x/pallas_call | solution.py:231
  1.8 31.3 %all_to_all.15 = f32[64,4,128]{2,1,0:T(4,128)S(1)} all-to-all(f32[64,4,128]{2,1,0:T(4,128)S(1)} %bitcast.9), channel_id=1, replica_groups=mesh['y'=8,'x1'=2,'x2'=4,'h'=16] {'x2','h'}, dimensions={0} | all-to-all | bytes 262144 | tf_op jit(solution)/shard_map/exchange_out/all_to_all | solution.py:253
  33.1 0.0 copy-start
  33.1 0.4 forward_y.1
  33.5 17.7 %all_to_all.16.sums = f32[16,16,256]{2,1,0:T(8,128)S(1)} all-to-all(f32[16,16,256]{2,1,0:T(8,128)S(1)} %get-tuple-element.18), channel_id=1, replica_groups={{0,128,112,240,256,384,368,496,512,640,624,752,768,896,880,1008},{16,14..., dimensions={0} | all-to-all | bytes 524288 | tf_op jit(solution)/shard_map/exchange_sums/all_to_all | solution.py:267
  51.2 0.0 copy-done
  51.2 0.4 inverse_y.1
  51.6 18.6 %all_to_all.17 = f32[64,4,128]{2,1,0:T(4,128)S(1)} all-to-all(f32[64,4,128]{2,1,0:T(4,128)S(1)} %bitcast.7), channel_id=1, replica_groups=mesh['y'=8,'x1'=2,'x2'=4,'h'=16] {'x2','h'}, dimensions={0} | all-to-all | bytes 262144 | tf_op jit(solution)/shard_map/exchange_back/all_to_all | solution.py:279
  70.3 0.9 %inverse_x.1 = f32[64,512]{1,0:T(8,128)} custom-call(f32[256,128]{1,0:T(8,128)S(1)} %bitcast.8, bf16[4,256,256]{2,1,0:T(8,128)(2,1)S(1)} %copy-done), custom_call_target="tpu_custom_call" | custom-call | tf_op jit(solution)/shard_map/inverse_x/pallas_call | solution.py:281
Async XLA Ops:
  33.1 18.1 %copy-start = (bf16[4,256,256]{2,1,0:T(8,128)(2,1)S(1)}, bf16[4,256,256]{2,1,0:T(8,128)(2,1)}, u32[]{:S(2)}) copy-start(bf16[4,256,256]{2,1,0:T(8,128)(2,1)} %constant.9.clone.table) | copy-start | bytes 1572868

commit v10 on v7

--- a/solution.py
+++ b/solution.py
@@ -120,7 +120,7 @@
         shift = shift + jnp.where(wave == e, eigen[first + e], 0.0)
 
     def inv(index):
-        part = 1.0 / jnp.full((8, 128), faces[index], F32)
+        part = pl.reciprocal(jnp.full((8, 128), faces[index], F32))
         part = jnp.concatenate([part, part], 1)
         return jnp.concatenate([part, part], 0)
 
@@ -150,7 +150,7 @@
         qs[c], ws[c] = q, w
         pa, pb, ua, ub = blocks[c]
         q, w = ub * q + pb * w, ua * q + pa * w
-    weight_out[...] = 1.0 / (p + last * u)
+    weight_out[...] = pl.reciprocal(p + last * u)
 
     me = own_block()
     inner = [inv(me * BLOCK + j) for j in range(BLOCK)]

time: 71.4 us -> 71.4 us (level)
  no operation moved by 1% of the time
where the time goes in v10:
time: 71.4 us; the launch traced here: 71.2 us
  blocking collectives  67.7 us (95%)
  Pallas kernels  3.49 us (5%)
    all_to_all x1, blocking collectives, on_device(): lax.all_to_all(half.reshape(BX * HA, 4, 128), ('x2', 'h'), 0, 0, tiled=True)  31.3 us
    all_to_all x1, blocking collectives, on_device(): lax.all_to_all(back.reshape(BX * HA, 4, 128), ('x2', 'h'), 0, 0, tiled=True)  18.7 us
    all_to_all x1, blocking collectives, on_device(): lax.all_to_all(sums, ('y', 'x1', 'x2'), 0, 0, tiled=True, axis_index_grou...  17.7 us
    pallas_call x1, Pallas kernels, on_device(): pl.pallas_call(forward_x, out_shape=(shape(M, 128), shape(BLOCK, 16, M),...  1.77 us

profile of v10, /device:TPU:1, one launch (start us, length us, event | category | flops | bytes accessed | tf_op | source)
XLA Modules:
  0.0 71.2 jit_solution(6904344637432023348)
XLA Ops:
  0.0 1.8 %forward_x.1 = (f32[256,128]{1,0:T(8,128)S(1)}, f32[8,16,256]{2,1,0:T(8,128)S(1)}, f32[8,16,256]{2,1,0:T(8,128)S(1)}, f32[16,256]{1,0:T(8,128)S(1)}, bf16[4,256,256]{2,1,0:T(8,128)(2,1)S(1)}) custom-call(f32[64,512]{1,0:T(8,128)} %bitcast.10, bf16[4,256,256]{2,1,0:T(8,128)(2,1)} %constant.8.clone.matrices, f32[129]{0:T(256)} %faces.1, ...), custom_call_target="tpu_custom_call" | custom-call | tf_op jit(solution)/shard_map/forward_x/pallas_call | solution.py:231
  1.8 31.3 %all_to_all.15 = f32[64,4,128]{2,1,0:T(4,128)S(1)} all-to-all(f32[64,4,128]{2,1,0:T(4,128)S(1)} %bitcast.9), channel_id=1, replica_groups=mesh['y'=8,'x1'=2,'x2'=4,'h'=16] {'x2','h'}, dimensions={0} | all-to-all | bytes 262144 | tf_op jit(solution)/shard_map/exchange_out/all_to_all | solution.py:253
  33.1 0.0 copy-start
  33.1 0.4 forward_y.1
  33.5 17.7 %all_to_all.16.sums = f32[16,16,256]{2,1,0:T(8,128)S(1)} all-to-all(f32[16,16,256]{2,1,0:T(8,128)S(1)} %get-tuple-element.18), channel_id=1, replica_groups={{0,128,256,384,512,640,768,896,112,240,368,496,624,752,880,1008},{16,14..., dimensions={0} | all-to-all | bytes 524288 | tf_op jit(solution)/shard_map/exchange_sums/all_to_all | solution.py:264
  51.2 0.0 copy-done
  51.2 0.4 inverse_y.1
  51.6 18.7 %all_to_all.17 = f32[64,4,128]{2,1,0:T(4,128)S(1)} all-to-all(f32[64,4,128]{2,1,0:T(4,128)S(1)} %bitcast.7), channel_id=1, replica_groups=mesh['y'=8,'x1'=2,'x2'=4,'h'=16] {'x2','h'}, dimensions={0} | all-to-all | bytes 262144 | tf_op jit(solution)/shard_map/exchange_back/all_to_all | solution.py:276
  70.3 0.9 %inverse_x.1 = f32[64,512]{1,0:T(8,128)} custom-call(f32[256,128]{1,0:T(8,128)S(1)} %bitcast.8, bf16[4,256,256]{2,1,0:T(8,128)(2,1)S(1)} %copy-done), custom_call_target="tpu_custom_call" | custom-call | tf_op jit(solution)/shard_map/inverse_x/pallas_call | solution.py:278
Async XLA Ops:
  33.1 18.1 %copy-start = (bf16[4,256,256]{2,1,0:T(8,128)(2,1)S(1)}, bf16[4,256,256]{2,1,0:T(8,128)(2,1)}, u32[]{:S(2)}) copy-start(bf16[4,256,256]{2,1,0:T(8,128)(2,1)} %constant.9.clone.table) | copy-start | bytes 1572868

commit v11 on v10

--- a/solution.py
+++ b/solution.py
@@ -77,7 +77,7 @@
 
 
 def forward_x(
-    source, matrices, faces, eigen, eigen_y, out, up_out, down_out, weight_out, table,
+    source, matrices, faces, eigen, eigen_y, out, up_out, down_out, table,
     value, face, wave_x, wave_y, ps, us, qs, ws, sems,
 ):
     copies = [
@@ -99,7 +99,7 @@
     half = jnp.concatenate([even, odd], 0).T
     for share in range(BX):
         out[pl.ds(place(share) * 64, 64)] = half[share * 64 : (share + 1) * 64]
-    coefficients(shift, blocks, inv, up_out, down_out, weight_out, ps, us, qs, ws)
+    coefficients(shift, blocks, inv, up_out, down_out, ps, us, qs, ws)
 
 
 def inverse_x(spectral, table, out):
@@ -138,7 +138,7 @@
     return shift, blocks, inv
 
 
-def coefficients(shift, blocks, inv, up_out, down_out, weight_out, ps, us, qs, ws):
+def coefficients(shift, blocks, inv, up_out, down_out, ps, us, qs, ws):
     last = inv(NZ)
     p, u = jnp.zeros((16, M), F32), jnp.ones((16, M), F32)
     q, w = last, jnp.ones((16, M), F32)
@@ -150,11 +150,11 @@
         qs[c], ws[c] = q, w
         pa, pb, ua, ub = blocks[c]
         q, w = ub * q + pb * w, ua * q + pa * w
-    weight_out[...] = pl.reciprocal(p + last * u)
+    weight = pl.reciprocal(p + last * u)
 
     me = own_block()
     inner = [inv(me * BLOCK + j) for j in range(BLOCK)]
-    p, u, q, w = ps[me], us[me], qs[me], ws[me]
+    p, u, q, w = ps[me], us[me], qs[me] * weight, ws[me] * weight
     for j in range(BLOCK):
         p = p + inner[j] * u
         up_out[j] = p
@@ -165,7 +165,7 @@
         q = q + inner[k] * w
 
 
-def forward_y(received, table, ups, downs, weight, local, sums):
+def forward_y(received, table, ups, downs, local, sums):
     value = received[...].reshape(BX, 2, 2, 16, 128)
     low, high = value[:, 0], value[:, 1]
 
@@ -178,8 +178,7 @@
     mask = lower_half((8, 8, M))
     lower = jnp.where(mask, even, pltpu.roll(odd, 4, 1)).reshape(BX, 16, M)
     upper = jnp.where(mask, pltpu.roll(even, 4, 1), odd).reshape(BX, 16, M)
-    scale = weight[...]
-    rows = [(lower if j % 2 == 0 else upper)[j // 2] * scale for j in range(BLOCK)]
+    rows = [(lower if j % 2 == 0 else upper)[j // 2] for j in range(BLOCK)]
     above = [None] * BLOCK
     total_q = jnp.zeros((16, M), F32)
     for j in reversed(range(BLOCK)):
@@ -228,17 +227,16 @@
     forward, inverse, eigen, eigen_y = (jnp.asarray(t) for t in tables())
     with jax.named_scope("forward_x"):
         operands = (source.reshape(64, N), forward, faces, eigen, eigen_y)
-        half, ups, downs, weight, table = pl.pallas_call(
+        half, ups, downs, table = pl.pallas_call(
             forward_x,
             out_shape=(
                 shape(M, 128),
                 shape(BLOCK, 16, M),
                 shape(BLOCK, 16, M),
-                shape(16, M),
                 jax.ShapeDtypeStruct((4, M, M), BF16),
             ),
             in_specs=[HBM] * 5,
-            out_specs=(VMEM,) * 5,
+            out_specs=(VMEM,) * 4,
             scratch_shapes=[
                 pltpu.VMEM((64, N), F32),
                 pltpu.SMEM((NZ + 1,), F32),
@@ -255,10 +253,10 @@
         local, sums = pl.pallas_call(
             forward_y,
             out_shape=(shape(BLOCK, 16, M), shape(BLOCKS, 16, M)),
-            in_specs=[VMEM] * 5,
+            in_specs=[VMEM] * 4,
             out_specs=(VMEM, VMEM),
             compiler_params=SMALL,
-        )(pencils.reshape(M, 128), table, ups, downs, weight)
+        )(pencils.reshape(M, 128), table, ups, downs)
     with jax.named_scope("exchange_sums"):
         groups = [[y * NX + x for x in (k, NX - 1 - k) for y in range(NY)] for k in range(BX)]
         sums = lax.all_to_all(

time: 71.4 us -> 71.4 us (level)
  no operation moved by 1% of the time
where the time goes in v11:
time: 71.4 us; the launch traced here: 71.2 us
  blocking collectives  67.7 us (95%)
  Pallas kernels  3.48 us (5%)
    all_to_all x1, blocking collectives, on_device(): lax.all_to_all(half.reshape(BX * HA, 4, 128), ('x2', 'h'), 0, 0, tiled=True)  31.3 us
    all_to_all x1, blocking collectives, on_device(): lax.all_to_all(back.reshape(BX * HA, 4, 128), ('x2', 'h'), 0, 0, tiled=True)  18.7 us
    all_to_all x1, blocking collectives, on_device(): lax.all_to_all(sums, ('y', 'x1', 'x2'), 0, 0, tiled=True, axis_index_grou...  17.7 us
    pallas_call x1, Pallas kernels, on_device(): pl.pallas_call(forward_x, out_shape=(shape(M, 128), shape(BLOCK, 16, M),...  1.76 us

profile of v11, /device:TPU:1, one launch (start us, length us, event | category | flops | bytes accessed | tf_op | source)
XLA Modules:
  0.0 71.2 jit_solution(5605964678301958650)
XLA Ops:
  0.0 1.8 %forward_x.1 = (f32[256,128]{1,0:T(8,128)S(1)}, f32[8,16,256]{2,1,0:T(8,128)S(1)}, f32[8,16,256]{2,1,0:T(8,128)S(1)}, bf16[4,256,256]{2,1,0:T(8,128)(2,1)S(1)}) custom-call(f32[64,512]{1,0:T(8,128)} %bitcast.10, bf16[4,256,256]{2,1,0:T(8,128)(2,1)} %constant.8.clone.matrices, f32[129]{0:T(256)} %faces.1, f32[512]{0:T(512)} %constant.10.clone.eigen, ...), custom_call_target="tpu_custom_call" | custom-call | tf_op jit(solution)/shard_map/forward_x/pallas_call | solution.py:230
  1.8 31.3 %all_to_all.15 = f32[64,4,128]{2,1,0:T(4,128)S(1)} all-to-all(f32[64,4,128]{2,1,0:T(4,128)S(1)} %bitcast.9), channel_id=1, replica_groups=mesh['y'=8,'x1'=2,'x2'=4,'h'=16] {'x2','h'}, dimensions={0} | all-to-all | bytes 262144 | tf_op jit(solution)/shard_map/exchange_out/all_to_all | solution.py:251
  33.1 0.0 copy-start
  33.1 0.4 forward_y.1
  33.5 17.7 %all_to_all.16.sums = f32[16,16,256]{2,1,0:T(8,128)S(1)} all-to-all(f32[16,16,256]{2,1,0:T(8,128)S(1)} %get-tuple-element.16), channel_id=1, replica_groups={{0,128,256,384,512,640,768,896,112,240,368,496,624,752,880,1008},{16,14..., dimensions={0} | all-to-all | bytes 524288 | tf_op jit(solution)/shard_map/exchange_sums/all_to_all | solution.py:262
  51.2 0.0 copy-done
  51.2 0.4 inverse_y.1
  51.6 18.7 %all_to_all.17 = f32[64,4,128]{2,1,0:T(4,128)S(1)} all-to-all(f32[64,4,128]{2,1,0:T(4,128)S(1)} %bitcast.7), channel_id=1, replica_groups=mesh['y'=8,'x1'=2,'x2'=4,'h'=16] {'x2','h'}, dimensions={0} | all-to-all | bytes 262144 | tf_op jit(solution)/shard_map/exchange_back/all_to_all | solution.py:274
  70.3 0.9 %inverse_x.1 = f32[64,512]{1,0:T(8,128)} custom-call(f32[256,128]{1,0:T(8,128)S(1)} %bitcast.8, bf16[4,256,256]{2,1,0:T(8,128)(2,1)S(1)} %copy-done), custom_call_target="tpu_custom_call" | custom-call | tf_op jit(solution)/shard_map/inverse_x/pallas_call | solution.py:276
Async XLA Ops:
  33.1 18.1 %copy-start = (bf16[4,256,256]{2,1,0:T(8,128)(2,1)S(1)}, bf16[4,256,256]{2,1,0:T(8,128)(2,1)}, u32[]{:S(2)}) copy-start(bf16[4,256,256]{2,1,0:T(8,128)(2,1)} %constant.9.clone.table) | copy-start | bytes 1572868

commit v12 on v11

--- a/solution.py
+++ b/solution.py
@@ -125,12 +125,12 @@
         return jnp.concatenate([part, part], 0)
 
     blocks = [None] * BLOCKS
-    for b in range(0, BLOCKS, 2):
-        for c in (b, b + 1):
+    for b in range(0, BLOCKS, 4):
+        for c in range(b, b + 4):
             g = inv(c * BLOCK)
             blocks[c] = (jnp.ones((16, M), F32), g, shift, 1.0 + shift * g)
         for j in range(1, BLOCK):
-            for c in (b, b + 1):
+            for c in range(b, b + 4):
                 pa, pb, ua, ub = blocks[c]
                 g = inv(c * BLOCK + j)
                 pa, pb = pa + g * ua, pb + g * ub

time: 71.4 us -> 71.5 us (level)
  no operation moved by 1% of the time
where the time goes in v12:
time: 71.5 us; the launch traced here: 71.2 us
  blocking collectives  67.7 us (95%)
  Pallas kernels  3.52 us (5%)
    all_to_all x1, blocking collectives, on_device(): lax.all_to_all(half.reshape(BX * HA, 4, 128), ('x2', 'h'), 0, 0, tiled=True)  31.3 us
    all_to_all x1, blocking collectives, on_device(): lax.all_to_all(back.reshape(BX * HA, 4, 128), ('x2', 'h'), 0, 0, tiled=True)  18.7 us
    all_to_all x1, blocking collectives, on_device(): lax.all_to_all(sums, ('y', 'x1', 'x2'), 0, 0, tiled=True, axis_index_grou...  17.7 us
    pallas_call x1, Pallas kernels, on_device(): pl.pallas_call(forward_x, out_shape=(shape(M, 128), shape(BLOCK, 16, M),...  1.8 us

profile of v12, /device:TPU:1, one launch (start us, length us, event | category | flops | bytes accessed | tf_op | source)
XLA Modules:
  0.0 71.2 jit_solution(1037137755107782031)
XLA Ops:
  0.0 1.8 %forward_x.1 = (f32[256,128]{1,0:T(8,128)S(1)}, f32[8,16,256]{2,1,0:T(8,128)S(1)}, f32[8,16,256]{2,1,0:T(8,128)S(1)}, bf16[4,256,256]{2,1,0:T(8,128)(2,1)S(1)}) custom-call(f32[64,512]{1,0:T(8,128)} %bitcast.10, bf16[4,256,256]{2,1,0:T(8,128)(2,1)} %constant.8.clone.matrices, f32[129]{0:T(256)} %faces.1, f32[512]{0:T(512)} %constant.10.clone.eigen, ...), custom_call_target="tpu_custom_call" | custom-call | tf_op jit(solution)/shard_map/forward_x/pallas_call | solution.py:230
  1.8 31.3 %all_to_all.15 = f32[64,4,128]{2,1,0:T(4,128)S(1)} all-to-all(f32[64,4,128]{2,1,0:T(4,128)S(1)} %bitcast.9), channel_id=1, replica_groups=mesh['y'=8,'x1'=2,'x2'=4,'h'=16] {'x2','h'}, dimensions={0} | all-to-all | bytes 262144 | tf_op jit(solution)/shard_map/exchange_out/all_to_all | solution.py:251
  33.1 0.0 copy-start
  33.1 0.4 forward_y.1
  33.5 17.7 %all_to_all.16.sums = f32[16,16,256]{2,1,0:T(8,128)S(1)} all-to-all(f32[16,16,256]{2,1,0:T(8,128)S(1)} %get-tuple-element.16), channel_id=1, replica_groups={{0,128,256,384,512,640,768,896,112,240,368,496,624,752,880,1008},{16,14..., dimensions={0} | all-to-all | bytes 524288 | tf_op jit(solution)/shard_map/exchange_sums/all_to_all | solution.py:262
  51.2 0.0 copy-done
  51.2 0.4 inverse_y.1
  51.7 18.7 %all_to_all.17 = f32[64,4,128]{2,1,0:T(4,128)S(1)} all-to-all(f32[64,4,128]{2,1,0:T(4,128)S(1)} %bitcast.7), channel_id=1, replica_groups=mesh['y'=8,'x1'=2,'x2'=4,'h'=16] {'x2','h'}, dimensions={0} | all-to-all | bytes 262144 | tf_op jit(solution)/shard_map/exchange_back/all_to_all | solution.py:274
  70.3 0.9 %inverse_x.1 = f32[64,512]{1,0:T(8,128)} custom-call(f32[256,128]{1,0:T(8,128)S(1)} %bitcast.8, bf16[4,256,256]{2,1,0:T(8,128)(2,1)S(1)} %copy-done), custom_call_target="tpu_custom_call" | custom-call | tf_op jit(solution)/shard_map/inverse_x/pallas_call | solution.py:276
Async XLA Ops:
  33.1 18.1 %copy-start = (bf16[4,256,256]{2,1,0:T(8,128)(2,1)S(1)}, bf16[4,256,256]{2,1,0:T(8,128)(2,1)}, u32[]{:S(2)}) copy-start(bf16[4,256,256]{2,1,0:T(8,128)(2,1)} %constant.9.clone.table) | copy-start | bytes 1572868
